TPU v7x, 128 devices: a whole 4x4x4 slice. The times are simulated.
128 devices in a mesh: blk: 4 (over z_hi, core), group: 32 (over y, x, z_lo).
Axes of the slice: x: 4, y: 4, z: 4 (z_hi: 2, z_lo: 2; z = z_hi * 2 + z_lo), core: 2. Of those that a mesh axis runs over, the one named last changes fastest.
Arguments:
- image_embed: float32 [16384, 768], P(('blk', 'group')), may hold values from -0.25 to 0.25
- text_embed: float32 [16384, 768], P(('blk', 'group')), may hold values from -0.25 to 0.25
- log_temp: float32 [1], replicated, may hold values from 1.8 to 2.6
- bias: float32 [1], replicated, may hold values from -9 to -7
Outputs:
- image_grad: float32 [16384, 768], P(('blk', 'group'))
- text_grad: float32 [16384, 768], P(('blk', 'group'))
- scalars: float32 [3], replicated
All inputs are finite; a program needn't handle non-finite values.
Results may differ from a plain program's by a relative error of at most 0.00045.
Values sent between devices are 32-bit elements; how exact they have to be, the bound alone decides.
No kernel may reach another device: no remote copies, remote signals or barrier semaphores. Data moves between devices by JAX's collectives and lax.ppermute only.
A program may use at most 128 MiB of HBM per device.

v0:
```python
import jax
import jax.numpy as jnp
from jax import lax
from jax.sharding import PartitionSpec as P

EPS = 1e-06


def unit_rows(embed):
    scale = lax.rsqrt(jnp.sum(embed * embed, axis=1, keepdims=True) + EPS)
    return (embed * scale, scale)


def body(image_embed, text_embed, log_temp, bias):
    rows = image_embed.shape[0]
    n_blk = lax.axis_size("blk")
    n_group = lax.axis_size("group")
    total = rows * n_blk * n_group
    blk_pos = lax.axis_index("blk")
    grp_pos = lax.axis_index("group")
    img_unit, img_scale = unit_rows(image_embed)
    txt_unit, txt_scale = unit_rows(text_embed)
    temp = jnp.exp(log_temp[0])
    shift = bias[0]
    img_set = lax.all_gather(img_unit, "blk", axis=0, tiled=True)
    set_rows = img_set.shape[0]
    set_ids = jnp.arange(set_rows, dtype=jnp.int32)
    img_key = jnp.where(set_ids // rows == blk_pos, grp_pos * rows + set_ids % rows, -1)
    piece = lax.all_gather(txt_unit, "group", axis=0, tiled=True)
    cols = jnp.arange(piece.shape[0], dtype=jnp.int32)
    sign = jnp.where(img_key[:, None] == cols[None, :], 1.0, -1.0).astype(jnp.float32)
    dots = lax.dot_general(
        img_set,
        piece,
        (((1,), (1,)), ((), ())),
        precision=lax.Precision.HIGHEST,
        preferred_element_type=jnp.float32,
    )
    logits = temp * dots + shift
    coef = -sign * jax.nn.sigmoid(-sign * logits)
    grad_img_acc = jnp.dot(
        coef, piece, precision=lax.Precision.HIGHEST, preferred_element_type=jnp.float32
    )
    txt_part = lax.dot_general(
        coef,
        img_set,
        (((0,), (0,)), ((), ())),
        precision=lax.Precision.HIGHEST,
        preferred_element_type=jnp.float32,
    )
    loss_acc = jnp.sum(jax.nn.softplus(-sign * logits))
    temp_acc = jnp.sum(coef * (logits - shift))
    bias_acc = jnp.sum(coef)
    img_acc, txt_buf, loss_sum, temp_acc, bias_acc = (
        grad_img_acc,
        txt_part,
        loss_acc,
        temp_acc,
        bias_acc,
    )
    txt_dir = temp * lax.psum_scatter(txt_buf, "group", scatter_dimension=0, tiled=True)
    img_dir = temp * lax.psum_scatter(img_acc, "blk", scatter_dimension=0, tiled=True)
    loss_all, temp_all, bias_all = lax.psum((loss_sum, temp_acc, bias_acc), ("blk", "group"))
    image_grad = img_scale * (
        img_dir - img_unit * jnp.sum(img_unit * img_dir, axis=1, keepdims=True)
    )
    text_grad = txt_scale * (
        txt_dir - txt_unit * jnp.sum(txt_unit * txt_dir, axis=1, keepdims=True)
    )
    scalars = jnp.stack([loss_all, temp_all, bias_all]) / total
    return (image_grad, text_grad, scalars)


def solution(mesh):
    in_specs = (P(("blk", "group"), None), P(("blk", "group"), None), P(), P())
    out_specs = (P(("blk", "group"), None), P(("blk", "group"), None), P())
    return jax.shard_map(body, mesh=mesh, in_specs=in_specs, out_specs=out_specs, check_vma=False)
```

profile of v0, /device:TPU:1, one launch (start us, length us, event | category | flops | bytes accessed | tf_op | source)
XLA Modules:
  0.0 692.8 jit_solution(6527422059224062883)
XLA Ops:
  7.2 0.0 all-gather.3.cloned.1.call-start
  7.2 1.1 multiply_reduce_fusion.4
  8.3 1.8 broadcast_multiply_fusion.1
  10.2 0.0 all-gather.3.cloned.1.call-update
  10.2 0.0 all-gather.5.cloned.1.call-start
  10.2 1.1 multiply_reduce_fusion.3
  11.4 1.8 broadcast_multiply_fusion
  13.2 0.0 all-gather.5.cloned.1.call-update
  13.2 0.0 reduce-scatter.3.cloned.1.call-start
  14.6 23.2 %all-gather.3.cloned.1.call-done = f32[512,768]{1,0:T(8,128)} async-done(((f32[128,768]{1,0:T(8,128)}), f32[512,768]{1,0:T(8,128)}) %all-gather.3.cloned.1.call-update) | async-done | bytes 1572880 | tf_op jit(solution)/shard_map/all_gather | solution.py:25
  37.8 274.9 %all-gather.5.cloned.1.call-done = f32[4096,768]{1,0:T(8,128)} async-done(((f32[128,768]{1,0:T(8,128)}), f32[4096,768]{1,0:T(8,128)}) %all-gather.5.cloned.1.call-update) | async-done | bytes 12582928 | tf_op jit(solution)/shard_map/all_gather | solution.py:29
  312.7 32.2 %fusion = (f32[]{:T(128)}, f32[]{:T(128)}, f32[]{:T(128)}, f32[512,4096]{1,0:T(8,128)S(1)}) fusion(f32[]{:T(128)} %bitcast.11, f32[]{:T(128)} %bitcast, s32[512]{0:T(512)S(1)} %fusion.8, f32[512,768]{1,0:T(8,128)} %all-gather.3.cloned.1.call-done, f32[4096,768]{1,0:T(8,128)} %all-gather.5.cloned.1.call-done), kind=kOutput, calls=%fused_computation.1 | convolution fusion | flops 19371393024 | bytes 22546452 | tf_op jit(solution)/shard_map/dot_general | solution.py:32
  344.9 3.2 copy-done
  348.1 22.4 %fusion.12 = f32[512,768]{1,0:T(8,128)} fusion(f32[512,4096]{1,0:T(8,128)S(1)} %get-tuple-element.9, f32[4096,768]{1,0:T(8,128)S(1)} %copy-done.4), kind=kOutput, calls=%fused_computation.33 | convolution fusion | flops 19327352832 | bytes 22544384 | tf_op jit(solution)/shard_map/dot_general | solution.py:41
  370.5 0.0 reduce-scatter.3.cloned.1.call-update
  370.6 0.0 reduce-scatter.5.cloned.1.call-start
  370.6 24.9 %fusion.13 = f32[4096,768]{1,0:T(8,128)} fusion(f32[512,4096]{1,0:T(8,128)} %copy-done, f32[512,768]{1,0:T(8,128)S(1)} %copy-done.3), kind=kOutput, calls=%fused_computation.34 | convolution fusion | flops 19327352832 | bytes 22544384 | tf_op jit(solution)/shard_map/dot_general | solution.py:44
  395.6 74.1 %all-reduce = (f32[1]{0:T(128)}, f32[1]{0:T(128)}, f32[1]{0:T(128)}) all-reduce(f32[1]{0:T(128)} %bitcast.4, f32[1]{0:T(128)} %bitcast.3, f32[1]{0:T(128)} %bitcast.2), channel_id=1, replica_groups=mesh['blk'=4,'group'=32] {'blk','group'}, use_global_device_ids=true, to_apply=%region_11.12 | all-reduce | flops 3 | bytes 24 | tf_op jit(solution)/shard_map/psum | solution.py:63
  469.6 2.5 maximum_multiply_fusion
  472.2 1.2 multiply_reduce_fusion.2
  473.4 1.9 subtract_multiply_fusion.1
  475.2 208.0 %reduce-scatter.5.cloned.1.call-done = f32[128,768]{1,0:T(8,128)} async-done(((f32[4096,768]{1,0:T(8,128)}), f32[128,768]{1,0:T(8,128)}) %reduce-scatter.5.cloned.1.call-update) | async-done | bytes 393232 | tf_op jit(solution)/shard_map/reduce_scatter | solution.py:61
  683.2 1.2 multiply_reduce_fusion.1
  684.4 1.9 subtract_multiply_fusion
  (14 shorter events, 0.1 us)
Async XLA Ops:
  7.2 30.7 %all-gather.3.cloned.1.call-start = ((), (), s32[]{:S(2)}) async-start(), calls=%async_computation.2 | async-start | bytes 1966080 | tf_op jit(solution)/shard_map/all_gather | solution.py:25
  10.2 302.5 %all-gather.5.cloned.1.call-start = ((), (), s32[]{:S(2)}) async-start(), calls=%async_computation.3 | async-start | bytes 12976128 | tf_op jit(solution)/shard_map/all_gather | solution.py:29
  13.2 458.9 %reduce-scatter.3.cloned.1.call-start = ((), (), s32[]{:S(2)}) async-start(), calls=%async_computation.4 | async-start | bytes 1966080 | tf_op jit(solution)/shard_map/reduce_scatter | solution.py:62
  312.7 35.4 %copy-start.4 = (f32[4096,768]{1,0:T(8,128)S(1)}, f32[4096,768]{1,0:T(8,128)}, u32[]{:S(2)}) copy-start(f32[4096,768]{1,0:T(8,128)} %all-gather.5.cloned.1.call-done) | copy-start | bytes 37748740
  344.9 3.2 copy-start
  348.1 22.5 %copy-start.3 = (f32[512,768]{1,0:T(8,128)S(1)}, f32[512,768]{1,0:T(8,128)}, u32[]{:S(2)}) copy-start(f32[512,768]{1,0:T(8,128)} %all-gather.3.cloned.1.call-done) | copy-start | bytes 4718596
  370.6 312.6 %reduce-scatter.5.cloned.1.call-start = ((), (), s32[]{:S(2)}) async-start(), calls=%async_computation.5 | async-start | bytes 12976128 | tf_op jit(solution)/shard_map/reduce_scatter | solution.py:61
  395.5 76.6 %copy-start.1 = (f32[128,768]{1,0:T(8,128)S(1)}, f32[128,768]{1,0:T(8,128)}, u32[]{:S(2)}) copy-start(f32[128,768]{1,0:T(8,128)} %param.4) | copy-start | bytes 1179652
  395.5 287.7 %copy-start.2 = (f32[128,768]{1,0:T(8,128)S(1)}, f32[128,768]{1,0:T(8,128)}, u32[]{:S(2)}) copy-start(f32[128,768]{1,0:T(8,128)} %param.5) | copy-start | bytes 1179652
Sparse Core Ops, SparseCore 0:
  10.3 27.4 all-gather.2
  40.0 272.6 all-gather.4
  370.7 35.8 reduce-scatter.2
  409.0 274.1 reduce-scatter.4
where the time goes:
time: 693 us
  waiting for transfers between devices  506 us (73%)
  matrix products  79.5 us (11%)
  blocking collectives  74.1 us (11%)
  between operations  15.1 us (2%)
  other arithmetic  14.6 us (2%)
    all_gather x1, waiting for transfers between devices, body(): piece = lax.all_gather(txt_unit, 'group', axis=0, tiled=True)  275 us
    reduce_scatter x1, waiting for transfers between devices, body(): lax.psum_scatter(txt_buf, 'group', scatter_dimension=0, tiled=True)  208 us
    psum x1, blocking collectives, body(): lax.psum((loss_sum, temp_acc, bias_acc), ('blk', 'group'))  74.1 us
    dot_general x1, matrix products, body(): lax.dot_general(img_set, piece, (((1,), (1,)), ((), ())), precision=lax.P...  32.2 us
    dot_general x1, matrix products, body(): lax.dot_general(coef, img_set, (((0,), (0,)), ((), ())), precision=lax.Pr...  24.9 us
    all_gather x1, waiting for transfers between devices, body(): img_set = lax.all_gather(img_unit, 'blk', axis=0, tiled=True)  23.2 us
    dot_general x1, matrix products, body(): jnp.dot(coef, piece, precision=lax.Precision.HIGHEST, preferred_element_t...  22.4 us
  transfers between devices with their start and end apart: 4, of which 3 were waited for; matrix products, arithmetic and copies ran while one was open for 5% of the time, Pallas kernels for 0%

commit v1 on v0

v1 whole, which is shorter than its diff:
```python
import functools

import jax
import jax.numpy as jnp
import numpy as np
from jax import lax
from jax.experimental import pallas as pl
from jax.experimental.pallas import tpu as pltpu
from jax.sharding import Mesh, PartitionSpec as P

EPS = 1e-06
AXES = ("zh", "c", "y", "x", "zl")
SIZES = (2, 2, 4, 4, 2)
ROWS = 128
UNIT = 256
E = 768
CHUNKS = 8
CUTS = ((0, 88), (88, 176), (176, 256))
F32 = jnp.float32
BF16 = jnp.bfloat16


def pairs(move):
    out = []
    for here in range(128):
        zh, c, y, x, zl = (int(v) for v in np.unravel_index(here, SIZES))
        c, x, y, z = move(c, x, y, 2 * zh + zl)
        there = np.ravel_multi_index((z // 2, c, y, x, z % 2), SIZES)
        out.append((here, int(there)))
    return out


def image_mate(v):
    return v ^ 1


def text_mate(v):
    return (((v + 1) ^ 1) - 1) % 4


def across(dim):
    def move(c, x, y, z):
        at = [x, y, z]
        at[dim] = (image_mate if c == 0 else text_mate)(at[dim])
        return (c, *at)

    return pairs(move)


def other_core(a):
    return lax.ppermute(a, AXES, pairs(lambda c, x, y, z: (1 - c, x, y, z)))


def swap(dim, a):
    return lax.ppermute(a, AXES, across(dim))


def split(x):
    hi = x.astype(BF16)
    return hi, (x - hi.astype(F32)).astype(BF16)


def unit(x):
    return x * lax.rsqrt(jnp.sum(x * x, axis=1, keepdims=True) + EPS)


def mm(a, b, dims):
    return lax.dot_general(a, b, (dims, ((), ())), preferred_element_type=F32)


def mm3(a, b, dims):
    return mm(a[0], b[0], dims) + mm(a[0], b[1], dims) + mm(a[1], b[0], dims)


def fold(x):
    return jnp.sum(x.reshape(-1, 8, x.shape[-1]), axis=0)


SUB = 256


def block_kernel(par, core, *refs):
    d_refs, e_refs = refs[:CHUNKS], refs[CHUNKS : 2 * CHUNKS]
    keep, send, scal = refs[2 * CHUNKS : 2 * CHUNKS + 3]
    img, txt, ih, il, p_img, p_txt, zero, sums, in_sem, out_sem, z_sem, i_sem = refs[2 * CHUNKS + 3 :]
    c = core[0]
    temp, shift = par[0], par[1]

    @pl.when(c == 0)
    def _():
        for k in range(CHUNKS):
            pltpu.make_async_copy(d_refs[k].at[pl.ds(0, ROWS)], img.at[k], in_sem.at[0, k]).start()
        for k in range(CHUNKS):
            pltpu.make_async_copy(e_refs[k], txt.at[k], in_sem.at[1, k]).start()

    @pl.when(c == 1)
    def _():
        for k in range(CHUNKS):
            pltpu.make_async_copy(e_refs[k].at[pl.ds(ROWS, ROWS)], img.at[k], in_sem.at[0, k]).start()
        for k in range(CHUNKS):
            pltpu.make_async_copy(d_refs[k], txt.at[k], in_sem.at[1, k]).start()

    zero[...] = jnp.zeros_like(zero)
    p_img[...] = jnp.zeros_like(p_img)
    sums[...] = jnp.zeros_like(sums)
    for k in range(CHUNKS):
        pltpu.make_async_copy(d_refs[k].at[pl.ds(0, ROWS)], img.at[k], in_sem.at[0, k]).wait()
        hi, lo = split(unit(img[k]))
        ih[pl.ds(k * ROWS, ROWS)] = hi
        il[pl.ds(k * ROWS, ROWS)] = lo

    @pl.loop(0, CHUNKS)
    def _(k):
        pltpu.make_async_copy(d_refs[0], txt.at[k], in_sem.at[1, k]).wait()
        t = split(unit(txt[k]))
        total = None
        for s in range(CHUNKS * ROWS // SUB):
            rows = pl.ds(s * SUB, SUB)
            i = (ih[rows], il[rows])
            dots = mm3(i, t, ((1,), (1,)))
            logits = temp * dots + shift
            e = jnp.exp(logits)
            u = 1.0 + e
            r = 1.0 / u
            loss = jnp.log(u) + (e - (u - 1.0)) * r
            coef = e * r
            if s == 0:
                row = lax.broadcasted_iota(jnp.int32, (SUB, UNIT), 0)
                col = lax.broadcasted_iota(jnp.int32, (SUB, UNIT), 1)
                same = (row + c * ROWS == col) & (row < ROWS) & (k == 0)
                coef = jnp.where(same, -r, coef)
                loss = jnp.where(same, loss - logits, loss)
            sums[0] += fold(loss)
            sums[1] += fold(coef * dots)
            sums[2] += fold(coef)
            g = split(coef)
            p_img[rows] += mm3(g, t, ((1,), (0,)))
            part = mm3(g, i, ((0,), (0,)))
            total = part if total is None else total + part
        slot = k % 2

        @pl.when(k >= 2)
        def _():
            pltpu.make_async_copy(p_txt.at[slot], keep.at[0], out_sem.at[slot]).wait()

        p_txt[slot] = total * temp

        @pl.when(c == 0)
        def _():
            pltpu.make_async_copy(p_txt.at[slot], send.at[k], out_sem.at[slot]).start()

        @pl.when(c == 1)
        def _():
            pltpu.make_async_copy(p_txt.at[slot], keep.at[k], out_sem.at[slot]).start()

    p_img[...] = p_img[...] * temp

    for k in range(CHUNKS):
        mine = p_img.at[pl.ds(k * ROWS, ROWS)]

        @pl.when(c == 0)
        def _():
            pltpu.make_async_copy(mine, keep.at[k, pl.ds(0, ROWS)], i_sem.at[k]).start()
            pltpu.make_async_copy(zero, keep.at[k, pl.ds(ROWS, ROWS)], z_sem.at[k]).start()

        @pl.when(c == 1)
        def _():
            pltpu.make_async_copy(zero, send.at[k, pl.ds(0, ROWS)], z_sem.at[k]).start()
            pltpu.make_async_copy(mine, send.at[k, pl.ds(ROWS, ROWS)], i_sem.at[k]).start()

    scal[0] = sums[0]
    scal[1] = sums[1] * temp
    scal[2] = sums[2]
    for slot in range(2):
        pltpu.make_async_copy(p_txt.at[slot], keep.at[0], out_sem.at[slot]).wait()
    for k in range(CHUNKS):
        pltpu.make_async_copy(zero, keep.at[0, pl.ds(0, ROWS)], z_sem.at[k]).wait()
        pltpu.make_async_copy(zero, keep.at[0, pl.ds(0, ROWS)], i_sem.at[k]).wait()


def block(par, core, ds, es):
    hbm = pl.BlockSpec(memory_space=pl.ANY)
    smem = pl.BlockSpec(memory_space=pltpu.SMEM)
    wide = jax.ShapeDtypeStruct((CHUNKS, UNIT, E), F32)
    return pl.pallas_call(
        block_kernel,
        out_shape=(wide, wide, jax.ShapeDtypeStruct((3, 8, UNIT), F32)),
        in_specs=[smem, smem] + [hbm] * (2 * CHUNKS),
        out_specs=(hbm, hbm, pl.BlockSpec(memory_space=pltpu.VMEM)),
        scratch_shapes=[
            pltpu.VMEM((CHUNKS, ROWS, E), F32),
            pltpu.VMEM((CHUNKS, UNIT, E), F32),
            pltpu.VMEM((CHUNKS * ROWS, E), BF16),
            pltpu.VMEM((CHUNKS * ROWS, E), BF16),
            pltpu.VMEM((CHUNKS * ROWS, E), F32),
            pltpu.VMEM((2, UNIT, E), F32),
            pltpu.VMEM((ROWS, E), F32),
            pltpu.VMEM((3, 8, UNIT), F32),
            pltpu.SemaphoreType.DMA((2, CHUNKS)),
            pltpu.SemaphoreType.DMA((2,)),
            pltpu.SemaphoreType.DMA((CHUNKS,)),
            pltpu.SemaphoreType.DMA((CHUNKS,)),
        ],
        compiler_params=pltpu.CompilerParams(vmem_limit_bytes=48 * 1024 * 1024),
        cost_estimate=pl.CostEstimate(
            flops=18 * CHUNKS * ROWS * CHUNKS * UNIT * E,
            bytes_accessed=4 * 40 * UNIT * E,
            transcendentals=3 * CHUNKS * ROWS * CHUNKS * UNIT,
        ),
        name="pair_block",
    )(par, core, *ds, *es)


def gather(own):
    dx, dy, dz = swap(0, own), swap(1, own), swap(2, own)
    dxy, dyz, dzx = swap(1, dx), swap(2, dy), swap(0, dz)
    far = [swap(d, a[lo:hi]) for d, a, (lo, hi) in zip((2, 0, 1), (dxy, dyz, dzx), CUTS)]
    return [own, dx, dy, dz, dxy, dyz, dzx, jnp.concatenate(far)]


def scatter(q):
    own, dx, dy, dz, dxy, dyz, dzx, far = q
    two = []
    for d, a, (lo, hi) in zip((2, 0, 1), (dxy, dyz, dzx), CUTS):
        two.append(a.at[lo:hi].add(swap(d, far[lo:hi])))
    one = [a + swap(d, b) for d, a, b in zip((1, 2, 0), (dx, dy, dz), two)]
    for d, a in zip((0, 1, 2), one):
        own = own + swap(d, a)
    return own


def back(embed, direction):
    scale = lax.rsqrt(jnp.sum(embed * embed, axis=1, keepdims=True) + EPS)
    u = embed * scale
    return scale * (direction - u * jnp.sum(u * direction, axis=1, keepdims=True))


def body(image_embed, text_embed, log_temp, bias):
    c = lax.axis_index("c")
    total = image_embed.shape[0] * 128
    par = jnp.concatenate([jnp.exp(log_temp), bias])
    mine = jnp.where(c == 0, image_embed, text_embed)
    rec = other_core(jnp.where(c == 0, text_embed, image_embed))
    own = jnp.concatenate([jnp.where(c == 0, mine, rec), jnp.where(c == 0, rec, mine)])
    ds = gather(own)
    es = [other_core(d) for d in ds]
    keep, send, scal = block(par, c.astype(jnp.int32).reshape(1), ds, es)
    got = other_core(send)
    q = [keep[k] + got[k] for k in range(CHUNKS)]
    sums = lax.psum(jnp.sum(scal, axis=(1, 2)), AXES)
    acc = scatter(q)
    low, high = acc[:ROWS], acc[ROWS:]
    rec = other_core(jnp.where(c == 0, high, low))
    img_dir = jnp.where(c == 0, low, rec)
    txt_dir = jnp.where(c == 0, rec, high)
    return back(image_embed, img_dir), back(text_embed, txt_dir), sums / total


def solution(mesh):
    fine = Mesh(mesh.devices.reshape(SIZES), AXES)
    wide = P(AXES, None)
    return jax.shard_map(
        body, mesh=fine, in_specs=(wide, wide, P(), P()), out_specs=(wide, wide, P()), check_vma=False
    )
```

time: 693 us -> 225 us (0.32)
  waiting for transfers between devices: 506 us -> 53.8 us
  matrix products: 79.5 us -> 0 us
  Pallas kernels: 0 us -> 47.3 us
  starting transfers between devices: 0.16 us -> 43.6 us
  between operations: 15.1 us -> 2.26 us
  blocking collectives: 74.1 us -> 62.6 us
    all_gather x2 -> x0, waiting for transfers between devices: 298 us -> none  [the longest x1 275 us: body(): piece = lax.all_gather(txt_unit, 'group', axis=0, tiled=True)]
    reduce_scatter x2 -> x0, waiting for transfers between devices: 208 us -> none  [the longest x1 208 us: body(): lax.psum_scatter(txt_buf, 'group', scatter_dimension=0, tiled=True)]
    dot_general x3 -> x0, matrix products: 79.5 us -> none  [the longest x1 32.2 us: body(): lax.dot_general(img_set, piece, (((1,), (1,)), ((), ())), precision=lax.P...]
    ppermute x0 -> x29, waiting for transfers between devices: none -> 53.8 us  [the longest x18 39.4 us: swap(): return lax.ppermute(a, AXES, across(dim))]
    pallas_call x0 -> x1, Pallas kernels: none -> 47.3 us  [block(): pl.pallas_call(block_kernel, out_shape=(wide, wide, jax.ShapeDtypeStruct(...]
    ppermute x0 -> x29, starting transfers between devices: none -> 43.6 us  [the longest x18 39.2 us: swap(): return lax.ppermute(a, AXES, across(dim))]
    psum x1, blocking collectives: 74.1 us -> 62.6 us  [body(): sums = lax.psum(jnp.sum(scal, axis=(1, 2)), AXES)]
    add x0 -> x3, other arithmetic: none -> 9.8 us  [the longest x1 4.5 us: body(): q = [keep[k] + got[k] for k in range(CHUNKS)]]
  transfers between devices with their start and end apart: 4 -> 29, of which waited for: 3 -> 19; matrix products, arithmetic and copies ran while one was open for 5% -> 0% of each run, Pallas kernels for 0% -> 0%
where the time goes in v1:
time: 225 us
  blocking collectives  62.6 us (28%)
  waiting for transfers between devices  53.8 us (24%)
  Pallas kernels  47.3 us (21%)
  starting transfers between devices  43.6 us (19%)
  other arithmetic  14.4 us (6%)
  between operations  2.26 us (1%)
    psum x1, blocking collectives, body(): sums = lax.psum(jnp.sum(scal, axis=(1, 2)), AXES)  62.6 us
    pallas_call x1, Pallas kernels, block(): pl.pallas_call(block_kernel, out_shape=(wide, wide, jax.ShapeDtypeStruct(...  47.3 us
    ppermute x18, waiting for transfers between devices, swap(): return lax.ppermute(a, AXES, across(dim))  39.4 us
    ppermute x18, starting transfers between devices, swap(): return lax.ppermute(a, AXES, across(dim))  39.2 us
    ppermute x11, waiting for transfers between devices, other_core(): return lax.ppermute(a, AXES, pairs(lambda c, x, y, z: (1 - c, x, y, z)))  14.4 us
    add x1, other arithmetic, body(): q = [keep[k] + got[k] for k in range(CHUNKS)]  4.5 us
  transfers between devices with their start and end apart: 29, of which 19 were waited for; matrix products, arithmetic and copies ran while one was open for 0% of the time, Pallas kernels for 0%

profile of v1, /device:TPU:1, one launch (start us, length us, event | category | flops | bytes accessed | tf_op | source)
XLA Modules:
  0.0 225.1 jit_solution(11471753176120529568)
XLA Ops:
  5.9 2.6 %collective-permute-start.1 = (f32[256,768]{1,0:T(8,128)S(1)}, f32[256,768]{1,0:T(8,128)S(1)}, u32[]{:S(2)}, u32[]{:S(2)}) collective-permute-start(f32[256,768]{1,0:T(8,128)S(1)} %pad_maximum_fusion.refs_0_), channel_id=1, source_target_pairs={{0,2},{1,3},{2,0},{3,1},{4,6},{5,7},{6,4},{7,5},{8,10},{9,11},{10,... | collective-permute-start | bytes 2359304 | tf_op jit(solution)/shard_map/ppermute | solution.py:55
  8.5 2.7 %collective-permute-start.2 = (f32[256,768]{1,0:T(8,128)S(1)}, f32[256,768]{1,0:T(8,128)S(1)}, u32[]{:S(2)}, u32[]{:S(2)}) collective-permute-start(f32[256,768]{1,0:T(8,128)S(1)} %pad_maximum_fusion.refs_0_), channel_id=1, source_target_pairs={{0,8},{1,9},{2,10},{3,11},{4,12},{5,13},{6,14},{7,15},{8,0},{9,1},... | collective-permute-start | bytes 2359304 | tf_op jit(solution)/shard_map/ppermute | solution.py:55
  11.3 3.8 %collective-permute-start.3 = (f32[256,768]{1,0:T(8,128)S(1)}, f32[256,768]{1,0:T(8,128)S(1)}, u32[]{:S(2)}, u32[]{:S(2)}) collective-permute-start(f32[256,768]{1,0:T(8,128)S(1)} %pad_maximum_fusion.refs_0_), channel_id=1, source_target_pairs={{0,1},{1,0},{2,3},{3,2},{4,5},{5,4},{6,7},{7,6},{8,9},{9,8},{10,11... | collective-permute-start | bytes 2359304 | tf_op jit(solution)/shard_map/ppermute | solution.py:55
  15.0 3.0 %collective-permute-done.1.refs_1_ = f32[256,768]{1,0:T(8,128)S(1)} collective-permute-done((f32[256,768]{1,0:T(8,128)S(1)}, f32[256,768]{1,0:T(8,128)S(1)}, u32[]{:S(2)}, u32[]{:S(2)}) %collective-permute-start.1) | collective-permute-done | bytes 786464 | tf_op jit(solution)/shard_map/ppermute | solution.py:55
  18.0 2.8 %collective-permute-start.4 = (f32[256,768]{1,0:T(8,128)S(1)}, f32[256,768]{1,0:T(8,128)S(1)}, u32[]{:S(2)}, u32[]{:S(2)}) collective-permute-start(f32[256,768]{1,0:T(8,128)S(1)} %collective-permute-done.1.refs_1_), channel_id=1, source_target_pairs={{0,8},{1,9},{2,10},{3,11},{4,12},{5,13},{6,14},{7,15},{8,0},{9,1},... | collective-permute-start | bytes 2359304 | tf_op jit(solution)/shard_map/ppermute | solution.py:55
  20.8 3.8 %collective-permute-start.5 = (f32[256,768]{1,0:T(8,128)S(1)}, f32[256,768]{1,0:T(8,128)S(1)}, u32[]{:S(2)}, u32[]{:S(2)}) collective-permute-start(f32[256,768]{1,0:T(8,128)S(1)} %collective-permute-done.2.refs_2_), channel_id=1, source_target_pairs={{0,1},{1,0},{2,3},{3,2},{4,5},{5,4},{6,7},{7,6},{8,9},{9,8},{10,11... | collective-permute-start | bytes 2359304 | tf_op jit(solution)/shard_map/ppermute | solution.py:55
  24.6 2.5 %collective-permute-start.6 = (f32[256,768]{1,0:T(8,128)S(1)}, f32[256,768]{1,0:T(8,128)S(1)}, u32[]{:S(2)}, u32[]{:S(2)}) collective-permute-start(f32[256,768]{1,0:T(8,128)S(1)} %collective-permute-done.3.refs_3_), channel_id=1, source_target_pairs={{0,2},{1,3},{2,0},{3,1},{4,6},{5,7},{6,4},{7,5},{8,10},{9,11},{10,... | collective-permute-start | bytes 2359304 | tf_op jit(solution)/shard_map/ppermute | solution.py:55
  27.6 2.6 %collective-permute-done.4.refs_4_ = f32[256,768]{1,0:T(8,128)S(1)} collective-permute-done((f32[256,768]{1,0:T(8,128)S(1)}, f32[256,768]{1,0:T(8,128)S(1)}, u32[]{:S(2)}, u32[]{:S(2)}) %collective-permute-start.4) | collective-permute-done | bytes 786464 | tf_op jit(solution)/shard_map/ppermute | solution.py:55
  30.4 3.6 %collective-permute-done.5.refs_5_ = f32[256,768]{1,0:T(8,128)S(1)} collective-permute-done((f32[256,768]{1,0:T(8,128)S(1)}, f32[256,768]{1,0:T(8,128)S(1)}, u32[]{:S(2)}, u32[]{:S(2)}) %collective-permute-start.5) | collective-permute-done | bytes 786464 | tf_op jit(solution)/shard_map/ppermute | solution.py:55
  34.0 2.7 %collective-permute-start.7 = (f32[88,768]{1,0:T(8,128)S(1)}, f32[88,768]{1,0:T(8,128)S(1)}, u32[]{:S(2)}, u32[]{:S(2)}) collective-permute-start(f32[88,768]{1,0:T(8,128)S(1)} %slice.171), channel_id=1, source_target_pairs={{0,1},{1,0},{2,3},{3,2},{4,5},{5,4},{6,7},{7,6},{8,9},{9,8},{10,11... | collective-permute-start | bytes 811016 | tf_op jit(solution)/shard_map/ppermute | solution.py:55
  36.7 2.6 %collective-permute-start.8 = (f32[88,768]{1,0:T(8,128)S(1)}, f32[88,768]{1,0:T(8,128)S(1)}, u32[]{:S(2)}, u32[]{:S(2)}) collective-permute-start(f32[88,768]{1,0:T(8,128)S(1)} %slice.172), channel_id=1, source_target_pairs={{0,2},{1,3},{2,0},{3,1},{4,6},{5,7},{6,4},{7,5},{8,10},{9,11},{10,... | collective-permute-start | bytes 811016 | tf_op jit(solution)/shard_map/ppermute | solution.py:55
  40.5 2.5 %collective-permute-start.9 = (f32[80,768]{1,0:T(8,128)S(1)}, f32[80,768]{1,0:T(8,128)S(1)}, u32[]{:S(2)}, u32[]{:S(2)}) collective-permute-start(f32[80,768]{1,0:T(8,128)S(1)} %slice.173), channel_id=1, source_target_pairs={{0,8},{1,9},{2,10},{3,11},{4,12},{5,13},{6,14},{7,15},{8,0},{9,1},... | collective-permute-start | bytes 737288 | tf_op jit(solution)/shard_map/ppermute | solution.py:55
  43.3 3.4 %collective-permute-done.9 = f32[80,768]{1,0:T(8,128)S(1)} collective-permute-done((f32[80,768]{1,0:T(8,128)S(1)}, f32[80,768]{1,0:T(8,128)S(1)}, u32[]{:S(2)}, u32[]{:S(2)}) %collective-permute-start.9) | collective-permute-done | bytes 245792 | tf_op jit(solution)/shard_map/ppermute | solution.py:55
  53.3 47.3 %pair_block.1 = (f32[8,256,768]{2,1,0:T(8,128)}, f32[8,256,768]{2,1,0:T(8,128)}, f32[3,8,256]{2,1,0:T(8,128)S(1)}) custom-call(f32[2]{0:T(128)S(1)} %pad_maximum_fusion.1.par, s32[1]{0:T(128)} %bitcast.core, f32[256,768]{1,0:T(8,128)S(1)} %pad_maximum_fusion.refs_0_, f32[256,768]{1,0:T(8,128)S(1)} %collective-permute-done.1.refs_1_, ...), custom_call_target="tpu_custom_call" | custom-call | flops 28991029248 | bytes 31457280 | tf_op jit(solution)/shard_map/pair_block/pallas_call | solution.py:185
  101.7 10.0 %collective-permute-done.18 = f32[8,256,768]{2,1,0:T(8,128)S(1)} collective-permute-done((f32[8,256,768]{2,1,0:T(8,128)}, f32[8,256,768]{2,1,0:T(8,128)S(1)}, u32[]{:S(2)}, u32[]{:S(2)}) %collective-permute-start.18) | collective-permute-done | bytes 6291488 | tf_op jit(solution)/shard_map/ppermute | solution.py:51
  111.7 4.5 %slice_add_fusion.5 = (f32[1,256,768]{2,1,0:T(8,128)S(1)}, f32[1,256,768]{2,1,0:T(8,128)S(1)}, f32[1,256,768]{2,1,0:T(8,128)S(1)}, f32[1,256,768]{2,1,0:T(8,128)S(1)}) fusion(f32[8,256,768]{2,1,0:T(8,128)S(1)} %collective-permute-done.18, f32[8,256,768]{2,1,0:T(8,128)} %get-tuple-element.42), kind=kLoop, calls=%fused_computation.9 | loop fusion | flops 786432 | bytes 9437184 | tf_op jit(solution)/shard_map/add | solution.py:249
  116.2 2.6 %collective-permute-start.25 = (f32[80,768]{1,0:T(8,128)S(1)}, f32[80,768]{1,0:T(8,128)S(1)}, u32[]{:S(2)}, u32[]{:S(2)}) collective-permute-start(f32[80,768]{1,0:T(8,128)S(1)} %slice_bitcast_fusion.4), channel_id=1, source_target_pairs={{0,8},{1,9},{2,10},{3,11},{4,12},{5,13},{6,14},{7,15},{8,0},{9,1},... | collective-permute-start | bytes 737288 | tf_op jit(solution)/shard_map/ppermute | solution.py:55
  118.8 2.8 %collective-permute-start.19 = (f32[88,768]{1,0:T(8,128)S(1)}, f32[88,768]{1,0:T(8,128)S(1)}, u32[]{:S(2)}, u32[]{:S(2)}) collective-permute-start(f32[88,768]{1,0:T(8,128)S(1)} %get-tuple-element.58), channel_id=1, source_target_pairs={{0,1},{1,0},{2,3},{3,2},{4,5},{5,4},{6,7},{7,6},{8,9},{9,8},{10,11... | collective-permute-start | bytes 811016 | tf_op jit(solution)/shard_map/ppermute | solution.py:55
  122.6 2.5 %collective-permute-start.26 = (f32[256,768]{1,0:T(8,128)S(1)}, f32[256,768]{1,0:T(8,128)S(1)}, u32[]{:S(2)}, u32[]{:S(2)}) collective-permute-start(f32[256,768]{1,0:T(8,128)S(1)} %fusion.15), channel_id=1, source_target_pairs={{0,2},{1,3},{2,0},{3,1},{4,6},{5,7},{6,4},{7,5},{8,10},{9,11},{10,... | collective-permute-start | bytes 2359304 | tf_op jit(solution)/shard_map/ppermute | solution.py:55
  128.9 7.6 %collective-permute-done.26 = f32[256,768]{1,0:T(8,128)S(1)} collective-permute-done((f32[256,768]{1,0:T(8,128)S(1)}, f32[256,768]{1,0:T(8,128)S(1)}, u32[]{:S(2)}, u32[]{:S(2)}) %collective-permute-start.26) | collective-permute-done | bytes 786464 | tf_op jit(solution)/shard_map/ppermute | solution.py:55
  137.6 2.7 %collective-permute-done.23 = f32[256,768]{1,0:T(8,128)S(1)} collective-permute-done((f32[256,768]{1,0:T(8,128)S(1)}, f32[256,768]{1,0:T(8,128)S(1)}, u32[]{:S(2)}, u32[]{:S(2)}) %collective-permute-start.23) | collective-permute-done | bytes 786464 | tf_op jit(solution)/shard_map/ppermute | solution.py:55
  140.3 3.2 %fusion.5 = (f32[256,768]{1,0:T(8,128)}, f32[256,768]{1,0:T(8,128)}, f32[256,768]{1,0:T(8,128)S(1)}) fusion(f32[256,768]{1,0:T(8,128)S(1)} %collective-permute-done.20, f32[8,256,768]{2,1,0:T(8,128)S(1)} %collective-permute-done.18, f32[8,256,768]{2,1,0:T(8,128)} %get-tuple-element.42, f32[256,768]{1,0:T(8,128)S(1)} %collective-permute-done.26, ...), kind=kLoop, calls=%fused_computation.12 | loop fusion | flops 1179648 | bytes 9437184 | tf_op jit(solution)/shard_map/add | solution.py:226
  147.2 8.5 %collective-permute-done.21 = f32[256,768]{1,0:T(8,128)S(1)} collective-permute-done((f32[256,768]{1,0:T(8,128)}, f32[256,768]{1,0:T(8,128)S(1)}, u32[]{:S(2)}, u32[]{:S(2)}) %collective-permute-start.21) | collective-permute-done | bytes 786464 | tf_op jit(solution)/shard_map/ppermute | solution.py:55
  160.7 62.6 %psum.7 = f32[3]{0:T(128)S(1)} all-reduce(f32[3]{0:T(128)S(1)} %reduce_sum.49), channel_id=1, replica_groups=mesh['zh'=2,'c'=2,'y'=4,'x'=4,'zl'=2] {'zh','c','y','x','zl'}, use_global_device_ids=true, to_apply=%region_5.6 | all-reduce | flops 3 | bytes 24 | tf_op jit(solution)/shard_map/psum | solution.py:250
  (87 shorter events, 30.0 us)
Async XLA Ops:
  5.9 12.1 %collective-permute-start.1 = (f32[256,768]{1,0:T(8,128)S(1)}, f32[256,768]{1,0:T(8,128)S(1)}, u32[]{:S(2)}, u32[]{:S(2)}) collective-permute-start(f32[256,768]{1,0:T(8,128)S(1)} %pad_maximum_fusion.refs_0_), channel_id=1, source_target_pairs={{0,2},{1,3},{2,0},{3,1},{4,6},{5,7},{6,4},{7,5},{8,10},{9,11},{10,... | collective-permute-start | bytes 2359304 | tf_op jit(solution)/shard_map/ppermute | solution.py:55
  8.5 12.3 %collective-permute-start.2 = (f32[256,768]{1,0:T(8,128)S(1)}, f32[256,768]{1,0:T(8,128)S(1)}, u32[]{:S(2)}, u32[]{:S(2)}) collective-permute-start(f32[256,768]{1,0:T(8,128)S(1)} %pad_maximum_fusion.refs_0_), channel_id=1, source_target_pairs={{0,8},{1,9},{2,10},{3,11},{4,12},{5,13},{6,14},{7,15},{8,0},{9,1},... | collective-permute-start | bytes 2359304 | tf_op jit(solution)/shard_map/ppermute | solution.py:55
  11.3 13.3 %collective-permute-start.3 = (f32[256,768]{1,0:T(8,128)S(1)}, f32[256,768]{1,0:T(8,128)S(1)}, u32[]{:S(2)}, u32[]{:S(2)}) collective-permute-start(f32[256,768]{1,0:T(8,128)S(1)} %pad_maximum_fusion.refs_0_), channel_id=1, source_target_pairs={{0,1},{1,0},{2,3},{3,2},{4,5},{5,4},{6,7},{7,6},{8,9},{9,8},{10,11... | collective-permute-start | bytes 2359304 | tf_op jit(solution)/shard_map/ppermute | solution.py:55
  18.0 12.2 %collective-permute-start.4 = (f32[256,768]{1,0:T(8,128)S(1)}, f32[256,768]{1,0:T(8,128)S(1)}, u32[]{:S(2)}, u32[]{:S(2)}) collective-permute-start(f32[256,768]{1,0:T(8,128)S(1)} %collective-permute-done.1.refs_1_), channel_id=1, source_target_pairs={{0,8},{1,9},{2,10},{3,11},{4,12},{5,13},{6,14},{7,15},{8,0},{9,1},... | collective-permute-start | bytes 2359304 | tf_op jit(solution)/shard_map/ppermute | solution.py:55
  20.8 13.1 %collective-permute-start.5 = (f32[256,768]{1,0:T(8,128)S(1)}, f32[256,768]{1,0:T(8,128)S(1)}, u32[]{:S(2)}, u32[]{:S(2)}) collective-permute-start(f32[256,768]{1,0:T(8,128)S(1)} %collective-permute-done.2.refs_2_), channel_id=1, source_target_pairs={{0,1},{1,0},{2,3},{3,2},{4,5},{5,4},{6,7},{7,6},{8,9},{9,8},{10,11... | collective-permute-start | bytes 2359304 | tf_op jit(solution)/shard_map/ppermute | solution.py:55
  24.6 12.1 %collective-permute-start.6 = (f32[256,768]{1,0:T(8,128)S(1)}, f32[256,768]{1,0:T(8,128)S(1)}, u32[]{:S(2)}, u32[]{:S(2)}) collective-permute-start(f32[256,768]{1,0:T(8,128)S(1)} %collective-permute-done.3.refs_3_), channel_id=1, source_target_pairs={{0,2},{1,3},{2,0},{3,1},{4,6},{5,7},{6,4},{7,5},{8,10},{9,11},{10,... | collective-permute-start | bytes 2359304 | tf_op jit(solution)/shard_map/ppermute | solution.py:55
  27.1 19.7 %collective-permute-start.10 = (f32[256,768]{1,0:T(8,128)S(1)}, f32[256,768]{1,0:T(8,128)S(1)}, u32[]{:S(2)}, u32[]{:S(2)}) collective-permute-start(f32[256,768]{1,0:T(8,128)S(1)} %pad_maximum_fusion.refs_0_), channel_id=1, source_target_pairs={{0,32},{1,33},{2,34},{3,35},{4,36},{5,37},{6,38},{7,39},{8,40},{9,... | collective-permute-start | bytes 2359304 | tf_op jit(solution)/shard_map/ppermute | solution.py:51
  27.1 20.3 %collective-permute-start.13 = (f32[256,768]{1,0:T(8,128)S(1)}, f32[256,768]{1,0:T(8,128)S(1)}, u32[]{:S(2)}, u32[]{:S(2)}) collective-permute-start(f32[256,768]{1,0:T(8,128)S(1)} %collective-permute-done.3.refs_3_), channel_id=1, source_target_pairs={{0,32},{1,33},{2,34},{3,35},{4,36},{5,37},{6,38},{7,39},{8,40},{9,... | collective-permute-start | bytes 2359304 | tf_op jit(solution)/shard_map/ppermute | solution.py:51
  30.2 17.3 %collective-permute-start.12 = (f32[256,768]{1,0:T(8,128)S(1)}, f32[256,768]{1,0:T(8,128)S(1)}, u32[]{:S(2)}, u32[]{:S(2)}) collective-permute-start(f32[256,768]{1,0:T(8,128)S(1)} %collective-permute-done.2.refs_2_), channel_id=1, source_target_pairs={{0,32},{1,33},{2,34},{3,35},{4,36},{5,37},{6,38},{7,39},{8,40},{9,... | collective-permute-start | bytes 2359304 | tf_op jit(solution)/shard_map/ppermute | solution.py:51
  34.0 6.5 %collective-permute-start.7 = (f32[88,768]{1,0:T(8,128)S(1)}, f32[88,768]{1,0:T(8,128)S(1)}, u32[]{:S(2)}, u32[]{:S(2)}) collective-permute-start(f32[88,768]{1,0:T(8,128)S(1)} %slice.171), channel_id=1, source_target_pairs={{0,1},{1,0},{2,3},{3,2},{4,5},{5,4},{6,7},{7,6},{8,9},{9,8},{10,11... | collective-permute-start | bytes 811016 | tf_op jit(solution)/shard_map/ppermute | solution.py:55
  36.7 6.6 %collective-permute-start.8 = (f32[88,768]{1,0:T(8,128)S(1)}, f32[88,768]{1,0:T(8,128)S(1)}, u32[]{:S(2)}, u32[]{:S(2)}) collective-permute-start(f32[88,768]{1,0:T(8,128)S(1)} %slice.172), channel_id=1, source_target_pairs={{0,2},{1,3},{2,0},{3,1},{4,6},{5,7},{6,4},{7,5},{8,10},{9,11},{10,... | collective-permute-start | bytes 811016 | tf_op jit(solution)/shard_map/ppermute | solution.py:55
  40.5 6.3 %collective-permute-start.9 = (f32[80,768]{1,0:T(8,128)S(1)}, f32[80,768]{1,0:T(8,128)S(1)}, u32[]{:S(2)}, u32[]{:S(2)}) collective-permute-start(f32[80,768]{1,0:T(8,128)S(1)} %slice.173), channel_id=1, source_target_pairs={{0,8},{1,9},{2,10},{3,11},{4,12},{5,13},{6,14},{7,15},{8,0},{9,1},... | collective-permute-start | bytes 737288 | tf_op jit(solution)/shard_map/ppermute | solution.py:55
  43.3 6.1 %collective-permute-start.11 = (f32[256,768]{1,0:T(8,128)S(1)}, f32[256,768]{1,0:T(8,128)S(1)}, u32[]{:S(2)}, u32[]{:S(2)}) collective-permute-start(f32[256,768]{1,0:T(8,128)S(1)} %collective-permute-done.1.refs_1_), channel_id=1, source_target_pairs={{0,32},{1,33},{2,34},{3,35},{4,36},{5,37},{6,38},{7,39},{8,40},{9,... | collective-permute-start | bytes 2359304 | tf_op jit(solution)/shard_map/ppermute | solution.py:51
  100.6 11.0 %collective-permute-start.18 = (f32[8,256,768]{2,1,0:T(8,128)}, f32[8,256,768]{2,1,0:T(8,128)S(1)}, u32[]{:S(2)}, u32[]{:S(2)}) collective-permute-start(f32[8,256,768]{2,1,0:T(8,128)} %get-tuple-element.43), channel_id=1, source_target_pairs={{0,32},{1,33},{2,34},{3,35},{4,36},{5,37},{6,38},{7,39},{8,40},{9,... | collective-permute-start | bytes 18874376 | tf_op jit(solution)/shard_map/ppermute | solution.py:51
  116.2 6.4 %collective-permute-start.25 = (f32[80,768]{1,0:T(8,128)S(1)}, f32[80,768]{1,0:T(8,128)S(1)}, u32[]{:S(2)}, u32[]{:S(2)}) collective-permute-start(f32[80,768]{1,0:T(8,128)S(1)} %slice_bitcast_fusion.4), channel_id=1, source_target_pairs={{0,8},{1,9},{2,10},{3,11},{4,12},{5,13},{6,14},{7,15},{8,0},{9,1},... | collective-permute-start | bytes 737288 | tf_op jit(solution)/shard_map/ppermute | solution.py:55
  118.8 6.6 %collective-permute-start.19 = (f32[88,768]{1,0:T(8,128)S(1)}, f32[88,768]{1,0:T(8,128)S(1)}, u32[]{:S(2)}, u32[]{:S(2)}) collective-permute-start(f32[88,768]{1,0:T(8,128)S(1)} %get-tuple-element.58), channel_id=1, source_target_pairs={{0,1},{1,0},{2,3},{3,2},{4,5},{5,4},{6,7},{7,6},{8,9},{9,8},{10,11... | collective-permute-start | bytes 811016 | tf_op jit(solution)/shard_map/ppermute | solution.py:55
  121.5 6.5 %collective-permute-start.22 = (f32[88,768]{1,0:T(8,128)S(1)}, f32[88,768]{1,0:T(8,128)S(1)}, u32[]{:S(2)}, u32[]{:S(2)}) collective-permute-start(f32[88,768]{1,0:T(8,128)S(1)} %get-tuple-element.59), channel_id=1, source_target_pairs={{0,2},{1,3},{2,0},{3,1},{4,6},{5,7},{6,4},{7,5},{8,10},{9,11},{10,... | collective-permute-start | bytes 811016 | tf_op jit(solution)/shard_map/ppermute | solution.py:55
  122.6 13.9 %collective-permute-start.26 = (f32[256,768]{1,0:T(8,128)S(1)}, f32[256,768]{1,0:T(8,128)S(1)}, u32[]{:S(2)}, u32[]{:S(2)}) collective-permute-start(f32[256,768]{1,0:T(8,128)S(1)} %fusion.15), channel_id=1, source_target_pairs={{0,2},{1,3},{2,0},{3,1},{4,6},{5,7},{6,4},{7,5},{8,10},{9,11},{10,... | collective-permute-start | bytes 2359304 | tf_op jit(solution)/shard_map/ppermute | solution.py:55
  125.4 12.1 %collective-permute-start.20 = (f32[256,768]{1,0:T(8,128)S(1)}, f32[256,768]{1,0:T(8,128)S(1)}, u32[]{:S(2)}, u32[]{:S(2)}) collective-permute-start(f32[256,768]{1,0:T(8,128)S(1)} %fusion.13), channel_id=1, source_target_pairs={{0,8},{1,9},{2,10},{3,11},{4,12},{5,13},{6,14},{7,15},{8,0},{9,1},... | collective-permute-start | bytes 2359304 | tf_op jit(solution)/shard_map/ppermute | solution.py:55
  128.1 12.1 %collective-permute-start.23 = (f32[256,768]{1,0:T(8,128)S(1)}, f32[256,768]{1,0:T(8,128)S(1)}, u32[]{:S(2)}, u32[]{:S(2)}) collective-permute-start(f32[256,768]{1,0:T(8,128)S(1)} %fusion.11), channel_id=1, source_target_pairs={{0,1},{1,0},{2,3},{3,2},{4,5},{5,4},{6,7},{7,6},{8,9},{9,8},{10,11... | collective-permute-start | bytes 2359304 | tf_op jit(solution)/shard_map/ppermute | solution.py:55
  143.5 12.3 %collective-permute-start.21 = (f32[256,768]{1,0:T(8,128)}, f32[256,768]{1,0:T(8,128)S(1)}, u32[]{:S(2)}, u32[]{:S(2)}) collective-permute-start(f32[256,768]{1,0:T(8,128)} %get-tuple-element.47), channel_id=1, source_target_pairs={{0,2},{1,3},{2,0},{3,1},{4,6},{5,7},{6,4},{7,5},{8,10},{9,11},{10,... | collective-permute-start | bytes 2359304 | tf_op jit(solution)/shard_map/ppermute | solution.py:55
  144.3 12.4 %collective-permute-start.27 = (f32[256,768]{1,0:T(8,128)}, f32[256,768]{1,0:T(8,128)}, u32[]{:S(2)}, u32[]{:S(2)}) collective-permute-start(f32[256,768]{1,0:T(8,128)} %get-tuple-element.48), channel_id=1, source_target_pairs={{0,1},{1,0},{2,3},{3,2},{4,5},{5,4},{6,7},{7,6},{8,9},{9,8},{10,11... | collective-permute-start | bytes 2359304 | tf_op jit(solution)/shard_map/ppermute | solution.py:55
  146.3 12.2 %collective-permute-start.24 = (f32[256,768]{1,0:T(8,128)S(1)}, f32[256,768]{1,0:T(8,128)}, u32[]{:S(2)}, u32[]{:S(2)}) collective-permute-start(f32[256,768]{1,0:T(8,128)S(1)} %get-tuple-element.49), channel_id=1, source_target_pairs={{0,8},{1,9},{2,10},{3,11},{4,12},{5,13},{6,14},{7,15},{8,0},{9,1},... | collective-permute-start | bytes 2359304 | tf_op jit(solution)/shard_map/ppermute | solution.py:55
  160.6 63.2 %collective-permute-start.28 = (f32[128,768]{1,0:T(8,128)S(1)}, f32[128,768]{1,0:T(8,128)S(1)}, u32[]{:S(2)}, u32[]{:S(2)}) collective-permute-start(f32[128,768]{1,0:T(8,128)S(1)} %slice_select_fusion.1), channel_id=1, source_target_pairs={{0,32},{1,33},{2,34},{3,35},{4,36},{5,37},{6,38},{7,39},{8,40},{9,... | collective-permute-start | bytes 1179656 | tf_op jit(solution)/shard_map/ppermute | solution.py:51
  (17 other events, 269.2 us)

commit v2 on v0

v2 whole, which is shorter than its diff:
```python
import functools

import jax
import jax.numpy as jnp
import numpy as np
from jax import lax
from jax.experimental import pallas as pl
from jax.experimental.pallas import tpu as pltpu
from jax.sharding import Mesh, PartitionSpec as P

EPS = 1e-06
AXES = ("zh", "c", "y", "x", "zl")
SIZES = (2, 2, 4, 4, 2)
ROWS = 128
UNIT = 256
E = 768
CHUNKS = 8
NEAR = 4
HALF = NEAR * ROWS
SUB = 256
MIB = 1024 * 1024
F32 = jnp.float32
BF16 = jnp.bfloat16


def pairs(move):
    out = []
    for here in range(128):
        zh, c, y, x, zl = (int(v) for v in np.unravel_index(here, SIZES))
        c, x, y, z = move(c, x, y, 2 * zh + zl)
        there = np.ravel_multi_index((z // 2, c, y, x, z % 2), SIZES)
        out.append((here, int(there)))
    return out


def image_mate(v):
    return v ^ 1


def text_mate(v):
    return (((v + 1) ^ 1) - 1) % 4


def across(dim):
    def move(c, x, y, z):
        at = [x, y, z]
        at[dim] = (image_mate if c == 0 else text_mate)(at[dim])
        return (c, *at)

    return pairs(move)


def other_core(a):
    return lax.ppermute(a, AXES, pairs(lambda c, x, y, z: (1 - c, x, y, z)))


def swap(dim, a):
    return lax.ppermute(a, AXES, across(dim))


def split(x):
    hi = x.astype(BF16)
    return hi, (x - hi.astype(F32)).astype(BF16)


def unit(x):
    return x * lax.rsqrt(jnp.sum(x * x, axis=1, keepdims=True) + EPS)


def mm(a, b, dims):
    return lax.dot_general(a, b, (dims, ((), ())), preferred_element_type=F32)


def mm3(a, b, dims):
    return mm(a[0], b[0], dims) + mm(a[0], b[1], dims) + mm(a[1], b[0], dims)


def fold(x):
    return jnp.sum(x.reshape(-1, 8, x.shape[-1]), axis=0)


def prep_images(c, d_refs, e_refs, hi_ref, lo_ref):
    for k in range(NEAR):
        hi, lo = split(unit(jnp.where(c == 0, d_refs[k][:ROWS], e_refs[k][ROWS:])))
        hi_ref[pl.ds(k * ROWS, ROWS)] = hi
        lo_ref[pl.ds(k * ROWS, ROWS)] = lo


def prep_text(c, d_ref, e_ref, hi_ref, lo_ref, k):
    hi, lo = split(unit(jnp.where(c == 0, e_ref[...], d_ref[...])))
    hi_ref[k] = hi
    lo_ref[k] = lo


def work(par, ts, tasks, same, sums, totals):
    def image(j):
        rows = pl.ds(tasks[j][4], SUB)
        return tasks[j][1][rows], tasks[j][2][rows]

    n = len(tasks)
    totals = list(totals)
    ahead = mm3(image(0), ts[tasks[0][0]], ((1,), (1,)))
    coefs = None
    for j in range(n + 1):
        dots = ahead
        if j + 1 < n:
            ahead = mm3(image(j + 1), ts[tasks[j + 1][0]], ((1,), (1,)))
        if coefs is not None:
            at, _, _, partial, first = tasks[j - 1]
            partial[pl.ds(first, SUB)] += mm3(coefs, ts[at], ((1,), (0,)))
            part = mm3(coefs, image(j - 1), ((0,), (0,)))
            totals[at] = part if totals[at] is None else totals[at] + part
        if j < n:
            logits = par[0] * dots + par[1]
            e = jnp.exp(logits)
            u = 1.0 + e
            r = 1.0 / u
            loss = jnp.log(u) + (e - (u - 1.0)) * r
            coef = e * r
            if same is not None and j == 0:
                coef = jnp.where(same, -r, coef)
                loss = jnp.where(same, loss - logits, loss)
            sums[0] += fold(loss)
            sums[1] += fold(coef * dots)
            sums[2] += fold(coef)
            coefs = split(coef)
    return totals


def total_kernel(core, *refs):
    parts, mine, theirs = refs[:-2], refs[-2], refs[-1]

    def put(a, b):
        for half, dest in ((a, mine), (b, theirs)):
            rows = pl.ds(half * ROWS, ROWS)
            dest[...] = (parts[0][rows] + parts[1][rows]) + (parts[2][rows] + parts[3][rows]) + parts[4][rows]

    @pl.when(core[0] == 0)
    def _():
        put(0, 1)

    @pl.when(core[0] == 1)
    def _():
        put(1, 0)


def grad_of(embed, direction, out):
    scale = lax.rsqrt(jnp.sum(embed * embed, axis=1, keepdims=True) + EPS)
    u = embed * scale
    out[...] = scale * (direction - u * jnp.sum(u * direction, axis=1, keepdims=True))


def grad_kernel(par, core, image, text, mine, theirs, d_image, d_text):
    @pl.when(core[0] == 0)
    def _():
        grad_of(image[...], par[0] * mine[...], d_image)
        grad_of(text[...], par[0] * theirs[...], d_text)

    @pl.when(core[0] == 1)
    def _():
        grad_of(image[...], par[0] * theirs[...], d_image)
        grad_of(text[...], par[0] * mine[...], d_text)


def near_kernel(par, core, *refs):
    d_refs, e_refs = refs[:NEAR], refs[NEAR : 2 * NEAR]
    p_txt, p_img, ih, il, th, tl, sums = refs[2 * NEAR :]
    c = core[0]
    p_img[...] = jnp.zeros_like(p_img)
    sums[...] = jnp.zeros_like(sums)
    prep_images(c, d_refs, e_refs, ih, il)
    for k in range(NEAR):
        prep_text(c, d_refs[k], e_refs[k], th, tl, k)
    row = lax.broadcasted_iota(jnp.int32, (SUB, UNIT), 0)
    col = lax.broadcasted_iota(jnp.int32, (SUB, UNIT), 1)

    @pl.loop(0, NEAR // 2)
    def _(i):
        same = (row + c * ROWS == col) & (row < ROWS) & (i == 0)
        ts = [(th[2 * i + h], tl[2 * i + h]) for h in range(2)]
        tasks = [(h, ih, il, p_img, m * SUB) for h in range(2) for m in range(HALF // SUB)]
        out = work(par, ts, tasks, same, sums, [None, None])
        for h in range(2):
            p_txt[2 * i + h] = out[h]


def rest_kernel(par, core, *refs):
    d_refs, e_refs = refs[:NEAR], refs[NEAR : 2 * NEAR]
    p_txt, p_img, ihn, iln, thn, tln, i_sums = refs[2 * NEAR : 2 * NEAR + 7]
    outs = refs[2 * NEAR + 7 :]
    keep_far, send_far = outs[:NEAR], outs[NEAR : 2 * NEAR]
    keep_near, send_near, line, ihf, ilf, thf, tlf, pin, pif, sums = outs[2 * NEAR :]
    c = core[0]
    pin[...] = p_img[...]
    pif[...] = jnp.zeros_like(pif)
    sums[...] = i_sums[...]
    prep_images(c, d_refs, e_refs, ihf, ilf)
    for k in range(NEAR):
        prep_text(c, d_refs[k], e_refs[k], thf, tlf, k)

    def put(keep, send, total):
        @pl.when(c == 0)
        def _():
            send[...] = total

        @pl.when(c == 1)
        def _():
            keep[...] = total

    @pl.loop(0, NEAR // 2)
    def _(i):
        ts = [(thn[2 * i + h], tln[2 * i + h]) for h in range(2)]
        tasks = [(h, ihf, ilf, pif, m * SUB) for h in range(2) for m in range(HALF // SUB)]
        out = work(par, ts, tasks, None, sums, [p_txt[2 * i], p_txt[2 * i + 1]])
        for h in range(2):
            put(keep_near.at[2 * i + h], send_near.at[2 * i + h], out[h])

    @pl.loop(0, NEAR)
    def _(k):
        tasks = [(0, ihn, iln, pin, m * SUB) for m in range(HALF // SUB)]
        tasks += [(0, ihf, ilf, pif, m * SUB) for m in range(HALF // SUB)]
        total = work(par, [(thf[k], tlf[k])], tasks, None, sums, [None])[0]
        for j in range(NEAR):

            @pl.when(k == j)
            def _():
                put(keep_far[j], send_far[j], total)

    lane = lax.broadcasted_iota(jnp.int32, line.shape, 1)
    values = jnp.zeros(line.shape, F32)
    for j, factor in enumerate((1.0, par[0], 1.0)):
        values = jnp.where(lane == j, jnp.sum(sums[j]) * factor, values)
    line[...] = values
    blank = jnp.zeros((ROWS, E), F32)

    @pl.when(c == 0)
    def _():
        for k in range(NEAR):
            for src, dest in ((pin, keep_near.at[k]), (pif, keep_far[k])):
                dest[:ROWS] = src[pl.ds(k * ROWS, ROWS)]
                dest[ROWS:] = blank

    @pl.when(c == 1)
    def _():
        for k in range(NEAR):
            for src, dest in ((pin, send_near.at[k]), (pif, send_far[k])):
                dest[:ROWS] = blank
                dest[ROWS:] = src[pl.ds(k * ROWS, ROWS)]


SMEM = pl.BlockSpec(memory_space=pltpu.SMEM)
VMEM = pl.BlockSpec(memory_space=pltpu.VMEM)
SUMS = jax.ShapeDtypeStruct((3, 8, UNIT), F32)
CHUNK = jax.ShapeDtypeStruct((UNIT, E), F32)
FOUR = jax.ShapeDtypeStruct((NEAR, UNIT, E), F32)


def cost(pairs_done):
    return pl.CostEstimate(flops=0 * pairs_done, bytes_accessed=4 * UNIT * E, transcendentals=0)


def near_block(par, core, ds, es):
    image = jax.ShapeDtypeStruct((HALF, E), BF16)
    text = jax.ShapeDtypeStruct((NEAR, UNIT, E), BF16)
    return pl.pallas_call(
        near_kernel,
        out_shape=(FOUR, jax.ShapeDtypeStruct((HALF, E), F32), image, image, text, text, SUMS),
        in_specs=[SMEM, SMEM] + [VMEM] * (2 * NEAR),
        out_specs=(VMEM,) * 7,
        compiler_params=pltpu.CompilerParams(vmem_limit_bytes=16 * MIB),
        cost_estimate=cost(NEAR * NEAR * ROWS * UNIT),
        name="near_block",
    )(par, core, *ds, *es)


def rest_block(par, core, ds, es, before):
    image = pltpu.VMEM((HALF, E), BF16)
    text = pltpu.VMEM((NEAR, UNIT, E), BF16)
    return pl.pallas_call(
        rest_kernel,
        out_shape=(CHUNK,) * (2 * NEAR) + (FOUR, FOUR, jax.ShapeDtypeStruct((128, 128), F32)),
        in_specs=[SMEM, SMEM] + [VMEM] * (2 * NEAR + 7),
        out_specs=(VMEM,) * (2 * NEAR + 3),
        scratch_shapes=[image, image, text, text, pltpu.VMEM((HALF, E), F32), pltpu.VMEM((HALF, E), F32), pltpu.VMEM((3, 8, UNIT), F32)],
        compiler_params=pltpu.CompilerParams(vmem_limit_bytes=24 * MIB),
        cost_estimate=cost((CHUNKS * CHUNKS - NEAR * NEAR) * ROWS * UNIT),
        name="rest_block",
    )(par, core, *ds, *es, *before)


def small(kernel, scalars, arrays, rows, name):
    shape = jax.ShapeDtypeStruct((rows, E), F32)
    return pl.pallas_call(
        kernel,
        out_shape=(shape, shape),
        in_specs=[SMEM] * len(scalars) + [VMEM] * len(arrays),
        out_specs=(VMEM, VMEM),
        compiler_params=pltpu.CompilerParams(vmem_limit_bytes=8 * MIB),
        cost_estimate=cost(0),
        name=name,
    )(*scalars, *arrays)


def corner(a):
    def move(c, x, y, z):
        mate = image_mate if c == 0 else text_mate
        return (c, mate(x), mate(y), mate(z))

    return lax.ppermute(a, AXES, pairs(move))


def after(a, *others):
    return lax.optimization_barrier((a, *others))[0]


def all_sum(line):
    return jnp.sum(lax.all_to_all(line, AXES, 0, 0, tiled=True), axis=0)


def body(image_embed, text_embed, log_temp, bias):
    c = lax.axis_index("c")
    total = image_embed.shape[0] * 128
    temp = jnp.exp(log_temp)
    par = jnp.concatenate([temp, bias])
    core = c.astype(jnp.int32).reshape(1)
    img_rec, txt_rec = other_core(image_embed), other_core(text_embed)
    first = c == 0
    own = jnp.concatenate([jnp.where(first, image_embed, txt_rec), jnp.where(first, img_rec, text_embed)])
    e_own = jnp.concatenate([jnp.where(first, text_embed, img_rec), jnp.where(first, txt_rec, image_embed)])
    one = [swap(d, own) for d in range(3)]
    last = corner(after(own, *one))
    zx = swap(0, one[2])
    yz = swap(2, one[1])
    xy = swap(1, one[0])
    near, e_near = [own] + one, [e_own] + [other_core(after(a, *one)) for a in one]
    before = near_block(par, core, near, e_near)
    rest = [xy, yz, zx, last]
    e_rest = [other_core(after(a, before[-1], *rest)) for a in rest]
    outs = rest_block(par, core, rest, e_rest, before)
    keep, send, (keep_near, send_near, line) = outs[:NEAR], outs[NEAR : 2 * NEAR], outs[2 * NEAR :]
    q = [k + other_core(s) for k, s in zip(keep, send)]
    got = other_core(after(send_near, *q[:3]))
    q_near = [keep_near[k] + got[k] for k in range(NEAR)]
    two = [swap(d, a) for a, d in zip(q[:3], (1, 2, 0))]
    far = corner(after(q[3], *two))
    line = all_sum(after(line, *two))
    one = [swap(d, q_near[d + 1] + two[d]) for d in (2, 1, 0)]
    mine, theirs = small(total_kernel, (core,), (after(q_near[0], line), far, *one), ROWS, "total")
    theirs = other_core(theirs)
    d_image, d_text = small(grad_kernel, (par, core), (image_embed, text_embed, mine, theirs), ROWS, "grad")
    return d_image, d_text, line[:3] / total


def solution(mesh):
    fine = Mesh(mesh.devices.reshape(SIZES), AXES)
    wide = P(AXES, None)
    return jax.shard_map(
        body, mesh=fine, in_specs=(wide, wide, P(), P()), out_specs=(wide, wide, P()), check_vma=False
    )
```

time: 693 us -> 136 us (0.20)
  waiting for transfers between devices: 506 us -> 32.9 us
  matrix products: 79.5 us -> 0 us
  blocking collectives: 74.1 us -> 16 us
  Pallas kernels: 0 us -> 42.8 us
  starting transfers between devices: 0.16 us -> 33.7 us
  between operations: 15.1 us -> 2.11 us
  other arithmetic: 14.6 us -> 7.44 us
    all_gather x2 -> x0, waiting for transfers between devices: 298 us -> none  [the longest x1 275 us: body(): piece = lax.all_gather(txt_unit, 'group', axis=0, tiled=True)]
    reduce_scatter x2 -> x0, waiting for transfers between devices: 208 us -> none  [the longest x1 208 us: body(): lax.psum_scatter(txt_buf, 'group', scatter_dimension=0, tiled=True)]
    dot_general x3 -> x0, matrix products: 79.5 us -> none  [the longest x1 32.2 us: body(): lax.dot_general(img_set, piece, (((1,), (1,)), ((), ())), precision=lax.P...]
    psum x1 -> x0, blocking collectives: 74.1 us -> none  [body(): lax.psum((loss_sum, temp_acc, bias_acc), ('blk', 'group'))]
    pallas_call x0 -> x4, Pallas kernels: none -> 42.8 us  [the longest x1 28 us: rest_block(): pl.pallas_call(rest_kernel, out_shape=(CHUNK,) * (2 * NEAR) + (FOUR, FOUR...]
    ppermute x0 -> x29, starting transfers between devices: none -> 33.7 us  [the longest x12 20.1 us: swap(): return lax.ppermute(a, AXES, across(dim))]
    ppermute x0 -> x29, waiting for transfers between devices: none -> 32.9 us  [the longest x12 20.5 us: swap(): return lax.ppermute(a, AXES, across(dim))]
    all_to_all x0 -> x1, blocking collectives: none -> 16 us  [all_sum(): return jnp.sum(lax.all_to_all(line, AXES, 0, 0, tiled=True), axis=0)]
  transfers between devices with their start and end apart: 4 -> 29, of which waited for: 3 -> 18; matrix products, arithmetic and copies ran while one was open for 5% -> 5% of each run, Pallas kernels for 0% -> 8%
where the time goes in v2:
time: 136 us; the launch traced here: 135 us
  Pallas kernels  42.8 us (31%)
  starting transfers between devices  33.7 us (25%)
  waiting for transfers between devices  32.9 us (24%)
  blocking collectives  16 us (12%)
  other arithmetic  7.44 us (5%)
  between operations  2.11 us (2%)
    pallas_call x1, Pallas kernels, rest_block(): pl.pallas_call(rest_kernel, out_shape=(CHUNK,) * (2 * NEAR) + (FOUR, FOUR...  28 us
    ppermute x12, waiting for transfers between devices, swap(): return lax.ppermute(a, AXES, across(dim))  20.5 us
    ppermute x12, starting transfers between devices, swap(): return lax.ppermute(a, AXES, across(dim))  20.1 us
    all_to_all x1, blocking collectives, all_sum(): return jnp.sum(lax.all_to_all(line, AXES, 0, 0, tiled=True), axis=0)  16 us
    ppermute x15, waiting for transfers between devices, other_core(): return lax.ppermute(a, AXES, pairs(lambda c, x, y, z: (1 - c, x, y, z)))  12.4 us
    pallas_call x1, Pallas kernels, near_block(): pl.pallas_call(near_kernel, out_shape=(FOUR, jax.ShapeDtypeStruct((HALF,...  11.1 us
    ppermute x2, starting transfers between devices, corner(): return lax.ppermute(a, AXES, pairs(move))  8.53 us
    ppermute x15, starting transfers between devices, other_core(): return lax.ppermute(a, AXES, pairs(lambda c, x, y, z: (1 - c, x, y, z)))  5.06 us
  transfers between devices with their start and end apart: 29, of which 18 were waited for; matrix products, arithmetic and copies ran while one was open for 5% of the time, Pallas kernels for 8%

profile of v2, /device:TPU:1, one launch (start us, length us, event | category | flops | bytes accessed | tf_op | source)
XLA Modules:
  0.0 135.4 jit_solution(3213555429808808344)
XLA Ops:
  0.6 1.5 %collective-permute-start.1 = (f32[128,768]{1,0:T(8,128)}, f32[128,768]{1,0:T(8,128)S(1)}, u32[]{:S(2)}, u32[]{:S(2)}) collective-permute-start(f32[128,768]{1,0:T(8,128)} %image.1), channel_id=1, source_target_pairs={{0,32},{1,33},{2,34},{3,35},{4,36},{5,37},{6,38},{7,39},{8,40},{9,... | collective-permute-start | bytes 1179656 | tf_op jit(solution)/shard_map/ppermute | solution.py:54
  2.2 1.5 %collective-permute-done.1 = f32[128,768]{1,0:T(8,128)S(1)} collective-permute-done((f32[128,768]{1,0:T(8,128)}, f32[128,768]{1,0:T(8,128)S(1)}, u32[]{:S(2)}, u32[]{:S(2)}) %collective-permute-start.1) | collective-permute-done | bytes 393248 | tf_op jit(solution)/shard_map/ppermute | solution.py:54
  5.9 3.9 %collective-permute-start.6 = (f32[256,768]{1,0:T(8,128)S(1)}, f32[256,768]{1,0:T(8,128)S(1)}, u32[]{:S(2)}, u32[]{:S(2)}) collective-permute-start(f32[256,768]{1,0:T(8,128)S(1)} %pad_maximum_fusion.refs_0_), channel_id=1, source_target_pairs={{0,1},{1,0},{2,3},{3,2},{4,5},{5,4},{6,7},{7,6},{8,9},{9,8},{10,11... | collective-permute-start | bytes 2359304 | tf_op jit(solution)/shard_map/ppermute | solution.py:58
  9.8 2.7 %collective-permute-start.4 = (f32[256,768]{1,0:T(8,128)S(1)}, f32[256,768]{1,0:T(8,128)S(1)}, u32[]{:S(2)}, u32[]{:S(2)}) collective-permute-start(f32[256,768]{1,0:T(8,128)S(1)} %pad_maximum_fusion.refs_0_), channel_id=1, source_target_pairs={{0,8},{1,9},{2,10},{3,11},{4,12},{5,13},{6,14},{7,15},{8,0},{9,1},... | collective-permute-start | bytes 2359304 | tf_op jit(solution)/shard_map/ppermute | solution.py:58
  12.5 2.5 %collective-permute-start.2 = (f32[256,768]{1,0:T(8,128)S(1)}, f32[256,768]{1,0:T(8,128)S(1)}, u32[]{:S(2)}, u32[]{:S(2)}) collective-permute-start(f32[256,768]{1,0:T(8,128)S(1)} %pad_maximum_fusion.refs_0_), channel_id=1, source_target_pairs={{0,2},{1,3},{2,0},{3,1},{4,6},{5,7},{6,4},{7,5},{8,10},{9,11},{10,... | collective-permute-start | bytes 2359304 | tf_op jit(solution)/shard_map/ppermute | solution.py:58
  15.0 4.2 %collective-permute-done.6.refs_3_ = f32[256,768]{1,0:T(8,128)S(1)} collective-permute-done((f32[256,768]{1,0:T(8,128)S(1)}, f32[256,768]{1,0:T(8,128)S(1)}, u32[]{:S(2)}, u32[]{:S(2)}) %collective-permute-start.6) | collective-permute-done | bytes 786464 | tf_op jit(solution)/shard_map/ppermute | solution.py:58
  19.2 2.7 %collective-permute-done.4.refs_2_ = f32[256,768]{1,0:T(8,128)S(1)} collective-permute-done((f32[256,768]{1,0:T(8,128)S(1)}, f32[256,768]{1,0:T(8,128)S(1)}, u32[]{:S(2)}, u32[]{:S(2)}) %collective-permute-start.4) | collective-permute-done | bytes 786464 | tf_op jit(solution)/shard_map/ppermute | solution.py:58
  21.9 2.7 %collective-permute-done.2.refs_1_ = f32[256,768]{1,0:T(8,128)S(1)} collective-permute-done((f32[256,768]{1,0:T(8,128)S(1)}, f32[256,768]{1,0:T(8,128)S(1)}, u32[]{:S(2)}, u32[]{:S(2)}) %collective-permute-start.2) | collective-permute-done | bytes 786464 | tf_op jit(solution)/shard_map/ppermute | solution.py:58
  25.1 3.4 %collective-permute-start.8 = (f32[256,768]{1,0:T(8,128)S(1)}, f32[256,768]{1,0:T(8,128)S(1)}, u32[]{:S(2)}, u32[]{:S(2)}) collective-permute-start(f32[256,768]{1,0:T(8,128)S(1)} %pad_maximum_fusion.refs_0_), channel_id=1, source_target_pairs={{0,11},{1,10},{2,9},{3,8},{4,15},{5,14},{6,13},{7,12},{8,3},{9,2},... | collective-permute-start | bytes 2359304 | tf_op jit(solution)/shard_map/ppermute | solution.py:309
  29.9 2.7 %collective-permute-start.3 = (f32[256,768]{1,0:T(8,128)S(1)}, f32[256,768]{1,0:T(8,128)S(1)}, u32[]{:S(2)}, u32[]{:S(2)}) collective-permute-start(f32[256,768]{1,0:T(8,128)S(1)} %collective-permute-done.2.refs_1_), channel_id=1, source_target_pairs={{0,8},{1,9},{2,10},{3,11},{4,12},{5,13},{6,14},{7,15},{8,0},{9,1},... | collective-permute-start | bytes 2359304 | tf_op jit(solution)/shard_map/ppermute | solution.py:58
  34.0 11.1 %near_block.1 = (f32[4,256,768]{2,1,0:T(8,128)S(1)}, f32[512,768]{1,0:T(8,128)S(1)}, bf16[512,768]{1,0:T(8,128)(2,1)S(1)}, bf16[512,768]{1,0:T(8,128)(2,1)S(1)},...) custom-call(f32[2]{0:T(128)S(1)} %pad_maximum_fusion.2.par, ...), custom_call_target="tpu_custom_call" | custom-call | bytes 786432 | tf_op jit(solution)/shard_map/near_block/pallas_call | solution.py:265
  46.5 2.6 %collective-permute-done.5.refs_1_ = f32[256,768]{1,0:T(8,128)S(1)} collective-permute-done((f32[256,768]{1,0:T(8,128)S(1)}, f32[256,768]{1,0:T(8,128)S(1)}, u32[]{:S(2)}, u32[]{:S(2)}) %collective-permute-start.5) | collective-permute-done | bytes 786464 | tf_op jit(solution)/shard_map/ppermute | solution.py:58
  54.8 28.0 %rest_block.1 = (f32[256,768]{1,0:T(8,128)S(1)}, f32[256,768]{1,0:T(8,128)S(1)}, f32[256,768]{1,0:T(8,128)S(1)}, f32[256,768]{1,0:T(8,128)S(1)}, f32[256,768]{1,...) custom-call(f32[2]{0:T(128)S(1)} %pad_maximum_fusion.2.par, ...), custom_call_target="tpu_custom_call" | custom-call | bytes 786432 | tf_op jit(solution)/shard_map/rest_block/pallas_call | solution.py:279
  83.5 1.7 %collective-permute-done.16 = f32[256,768]{1,0:T(8,128)S(1)} collective-permute-done((f32[256,768]{1,0:T(8,128)S(1)}, f32[256,768]{1,0:T(8,128)S(1)}, u32[]{:S(2)}, u32[]{:S(2)}) %collective-permute-start.16) | collective-permute-done | bytes 786464 | tf_op jit(solution)/shard_map/ppermute | solution.py:54
  88.7 1.4 %collective-permute-start.21 = (f32[256,768]{1,0:T(8,128)S(1)}, f32[256,768]{1,0:T(8,128)S(1)}, u32[]{:S(2)}, u32[]{:S(2)}) collective-permute-start(f32[256,768]{1,0:T(8,128)S(1)} %add.46), channel_id=1, source_target_pairs={{0,1},{1,0},{2,3},{3,2},{4,5},{5,4},{6,7},{7,6},{8,9},{9,8},{10,11... | collective-permute-start | bytes 2359304 | tf_op jit(solution)/shard_map/ppermute | solution.py:58
  90.2 2.5 %collective-permute-start.22 = (f32[256,768]{1,0:T(8,128)S(1)}, f32[256,768]{1,0:T(8,128)S(1)}, u32[]{:S(2)}, u32[]{:S(2)}) collective-permute-start(f32[256,768]{1,0:T(8,128)S(1)} %add.47), channel_id=1, source_target_pairs={{0,2},{1,3},{2,0},{3,1},{4,6},{5,7},{6,4},{7,5},{8,10},{9,11},{10,... | collective-permute-start | bytes 2359304 | tf_op jit(solution)/shard_map/ppermute | solution.py:58
  92.7 1.7 %collective-permute-done.23 = f32[256,768]{1,0:T(8,128)S(1)} collective-permute-done((f32[256,768]{1,0:T(8,128)S(1)}, f32[256,768]{1,0:T(8,128)S(1)}, u32[]{:S(2)}, u32[]{:S(2)}) %collective-permute-start.23) | collective-permute-done | bytes 786464 | tf_op jit(solution)/shard_map/ppermute | solution.py:54
  95.3 4.8 %collective-permute-done.20 = f32[256,768]{1,0:T(8,128)S(1)} collective-permute-done((f32[256,768]{1,0:T(8,128)S(1)}, f32[256,768]{1,0:T(8,128)S(1)}, u32[]{:S(2)}, u32[]{:S(2)}) %collective-permute-start.20) | collective-permute-done | bytes 786464 | tf_op jit(solution)/shard_map/ppermute | solution.py:58
  100.8 1.4 %collective-permute-done.22 = f32[256,768]{1,0:T(8,128)S(1)} collective-permute-done((f32[256,768]{1,0:T(8,128)S(1)}, f32[256,768]{1,0:T(8,128)S(1)}, u32[]{:S(2)}, u32[]{:S(2)}) %collective-permute-start.22) | collective-permute-done | bytes 786464 | tf_op jit(solution)/shard_map/ppermute | solution.py:58
  102.3 5.2 %collective-permute-start.24 = (f32[256,768]{1,0:T(8,128)}, f32[256,768]{1,0:T(8,128)}, u32[]{:S(2)}, u32[]{:S(2)}) collective-permute-start(f32[256,768]{1,0:T(8,128)} %add.50), channel_id=1, source_target_pairs={{0,11},{1,10},{2,9},{3,8},{4,15},{5,14},{6,13},{7,12},{8,3},{9,2},... | collective-permute-start | bytes 2359304 | tf_op jit(solution)/shard_map/ppermute | solution.py:309
  107.4 2.0 %fusion.1 = (f32[256,768]{1,0:T(8,128)}, f32[256,768]{1,0:T(8,128)}, f32[256,768]{1,0:T(8,128)}) fusion(f32[256,768]{1,0:T(8,128)S(1)} %collective-permute-done.20, f32[4,256,768]{2,1,0:T(8,128)S(1)} %collective-permute-done.19, f32[4,256,768]{2,1,0:T(8,128)S(1)} %get-tuple-element.52, f32[256,768]{1,0:T(8,128)S(1)} %collective-permute-done.21, ...), kind=kLoop, calls=%fused_computation.2 | loop fusion | flops 1179648 | bytes 9437184 | tf_op jit(solution)/shard_map/add | solution.py:347
  112.2 16.0 %all_to_all.9 = f32[128,1,128]{2,1,0:T(1,128)S(1)} all-to-all(f32[128,1,128]{2,1,0:T(1,128)S(1)} %bitcast.18), channel_id=1, replica_groups=mesh['zh'=2,'c'=2,'y'=4,'x'=4,'zl'=2] {'zh','c','y','x','zl'}, dimensions={0} | all-to-all | bytes 131072 | tf_op jit(solution)/shard_map/all_to_all | solution.py:317
  129.6 2.0 %total.1 = (f32[128,768]{1,0:T(8,128)S(1)}, f32[128,768]{1,0:T(8,128)S(1)}) custom-call(s32[1]{0:T(128)} %bitcast.core, f32[256,768]{1,0:T(8,128)S(1)} %fusion.6.refs_0_, f32[256,768]{1,0:T(8,128)} %collective-permute-done.24.refs_1_, f32[256,768]{1,0:T(8,128)} %collective-permute-done.25.refs_2_, f32[256,768]{1,0:T(8,128)} %collective-permute-done.26.refs_3_, ...), custom_call_target="tpu_custom_call" | custom-call | bytes 786432 | tf_op jit(solution)/shard_map/total/pallas_call | solution.py:293
  133.7 1.7 %grad.1 = (f32[128,768]{1,0:T(8,128)}, f32[128,768]{1,0:T(8,128)}) custom-call(f32[2]{0:T(128)S(1)} %pad_maximum_fusion.2.par, s32[1]{0:T(128)} %bitcast.core, f32[128,768]{1,0:T(8,128)S(1)} %copy-done, f32[128,768]{1,0:T(8,128)S(1)} %copy-done.1, f32[128,768]{1,0:T(8,128)S(1)} %get-tuple-element.67.mine, f32[128,768]{1,0:T(8,128)S(1)} %collective-permute-done.28.theirs), custom_call_target="tpu_custom_call" | custom-call | bytes 786432 | tf_op jit(solution)/shard_map/grad/pallas_call | solution.py:293
  (58 shorter events, 23.5 us)
Async XLA Ops:
  5.9 13.3 %collective-permute-start.6 = (f32[256,768]{1,0:T(8,128)S(1)}, f32[256,768]{1,0:T(8,128)S(1)}, u32[]{:S(2)}, u32[]{:S(2)}) collective-permute-start(f32[256,768]{1,0:T(8,128)S(1)} %pad_maximum_fusion.refs_0_), channel_id=1, source_target_pairs={{0,1},{1,0},{2,3},{3,2},{4,5},{5,4},{6,7},{7,6},{8,9},{9,8},{10,11... | collective-permute-start | bytes 2359304 | tf_op jit(solution)/shard_map/ppermute | solution.py:58
  9.8 12.1 %collective-permute-start.4 = (f32[256,768]{1,0:T(8,128)S(1)}, f32[256,768]{1,0:T(8,128)S(1)}, u32[]{:S(2)}, u32[]{:S(2)}) collective-permute-start(f32[256,768]{1,0:T(8,128)S(1)} %pad_maximum_fusion.refs_0_), channel_id=1, source_target_pairs={{0,8},{1,9},{2,10},{3,11},{4,12},{5,13},{6,14},{7,15},{8,0},{9,1},... | collective-permute-start | bytes 2359304 | tf_op jit(solution)/shard_map/ppermute | solution.py:58
  12.5 12.1 %collective-permute-start.2 = (f32[256,768]{1,0:T(8,128)S(1)}, f32[256,768]{1,0:T(8,128)S(1)}, u32[]{:S(2)}, u32[]{:S(2)}) collective-permute-start(f32[256,768]{1,0:T(8,128)S(1)} %pad_maximum_fusion.refs_0_), channel_id=1, source_target_pairs={{0,2},{1,3},{2,0},{3,1},{4,6},{5,7},{6,4},{7,5},{8,10},{9,11},{10,... | collective-permute-start | bytes 2359304 | tf_op jit(solution)/shard_map/ppermute | solution.py:58
  24.6 4.1 %collective-permute-start.9 = (f32[256,768]{1,0:T(8,128)S(1)}, f32[256,768]{1,0:T(8,128)S(1)}, u32[]{:S(2)}, u32[]{:S(2)}) collective-permute-start(f32[256,768]{1,0:T(8,128)S(1)} %collective-permute-done.2.refs_1_), channel_id=1, source_target_pairs={{0,32},{1,33},{2,34},{3,35},{4,36},{5,37},{6,38},{7,39},{8,40},{9,... | collective-permute-start | bytes 2359304 | tf_op jit(solution)/shard_map/ppermute | solution.py:54
  24.6 5.3 %collective-permute-start.10 = (f32[256,768]{1,0:T(8,128)S(1)}, f32[256,768]{1,0:T(8,128)S(1)}, u32[]{:S(2)}, u32[]{:S(2)}) collective-permute-start(f32[256,768]{1,0:T(8,128)S(1)} %collective-permute-done.4.refs_2_), channel_id=1, source_target_pairs={{0,32},{1,33},{2,34},{3,35},{4,36},{5,37},{6,38},{7,39},{8,40},{9,... | collective-permute-start | bytes 2359304 | tf_op jit(solution)/shard_map/ppermute | solution.py:54
  25.1 8.9 %collective-permute-start.11 = (f32[256,768]{1,0:T(8,128)S(1)}, f32[256,768]{1,0:T(8,128)S(1)}, u32[]{:S(2)}, u32[]{:S(2)}) collective-permute-start(f32[256,768]{1,0:T(8,128)S(1)} %collective-permute-done.6.refs_3_), channel_id=1, source_target_pairs={{0,32},{1,33},{2,34},{3,35},{4,36},{5,37},{6,38},{7,39},{8,40},{9,... | collective-permute-start | bytes 2359304 | tf_op jit(solution)/shard_map/ppermute | solution.py:54
  25.1 24.1 %collective-permute-start.8 = (f32[256,768]{1,0:T(8,128)S(1)}, f32[256,768]{1,0:T(8,128)S(1)}, u32[]{:S(2)}, u32[]{:S(2)}) collective-permute-start(f32[256,768]{1,0:T(8,128)S(1)} %pad_maximum_fusion.refs_0_), channel_id=1, source_target_pairs={{0,11},{1,10},{2,9},{3,8},{4,15},{5,14},{6,13},{7,12},{8,3},{9,2},... | collective-permute-start | bytes 2359304 | tf_op jit(solution)/shard_map/ppermute | solution.py:309
  28.5 18.0 %collective-permute-start.7 = (f32[256,768]{1,0:T(8,128)S(1)}, f32[256,768]{1,0:T(8,128)S(1)}, u32[]{:S(2)}, u32[]{:S(2)}) collective-permute-start(f32[256,768]{1,0:T(8,128)S(1)} %collective-permute-done.6.refs_3_), channel_id=1, source_target_pairs={{0,2},{1,3},{2,0},{3,1},{4,6},{5,7},{6,4},{7,5},{8,10},{9,11},{10,... | collective-permute-start | bytes 2359304 | tf_op jit(solution)/shard_map/ppermute | solution.py:58
  28.7 20.5 %collective-permute-start.5 = (f32[256,768]{1,0:T(8,128)S(1)}, f32[256,768]{1,0:T(8,128)S(1)}, u32[]{:S(2)}, u32[]{:S(2)}) collective-permute-start(f32[256,768]{1,0:T(8,128)S(1)} %collective-permute-done.4.refs_2_), channel_id=1, source_target_pairs={{0,1},{1,0},{2,3},{3,2},{4,5},{5,4},{6,7},{7,6},{8,9},{9,8},{10,11... | collective-permute-start | bytes 2359304 | tf_op jit(solution)/shard_map/ppermute | solution.py:58
  29.9 19.3 %collective-permute-start.3 = (f32[256,768]{1,0:T(8,128)S(1)}, f32[256,768]{1,0:T(8,128)S(1)}, u32[]{:S(2)}, u32[]{:S(2)}) collective-permute-start(f32[256,768]{1,0:T(8,128)S(1)} %collective-permute-done.2.refs_1_), channel_id=1, source_target_pairs={{0,8},{1,9},{2,10},{3,11},{4,12},{5,13},{6,14},{7,15},{8,0},{9,1},... | collective-permute-start | bytes 2359304 | tf_op jit(solution)/shard_map/ppermute | solution.py:58
  49.2 3.4 %collective-permute-start.13 = (f32[256,768]{1,0:T(8,128)S(1)}, f32[256,768]{1,0:T(8,128)S(1)}, u32[]{:S(2)}, u32[]{:S(2)}) collective-permute-start(f32[256,768]{1,0:T(8,128)S(1)} %collective-permute-done.5.refs_1_), channel_id=1, source_target_pairs={{0,32},{1,33},{2,34},{3,35},{4,36},{5,37},{6,38},{7,39},{8,40},{9,... | collective-permute-start | bytes 2359304 | tf_op jit(solution)/shard_map/ppermute | solution.py:54
  49.7 4.0 %collective-permute-start.14 = (f32[256,768]{1,0:T(8,128)S(1)}, f32[256,768]{1,0:T(8,128)S(1)}, u32[]{:S(2)}, u32[]{:S(2)}) collective-permute-start(f32[256,768]{1,0:T(8,128)S(1)} %collective-permute-done.7.refs_2_), channel_id=1, source_target_pairs={{0,32},{1,33},{2,34},{3,35},{4,36},{5,37},{6,38},{7,39},{8,40},{9,... | collective-permute-start | bytes 2359304 | tf_op jit(solution)/shard_map/ppermute | solution.py:54
  49.7 5.1 %collective-permute-start.15 = (f32[256,768]{1,0:T(8,128)S(1)}, f32[256,768]{1,0:T(8,128)S(1)}, u32[]{:S(2)}, u32[]{:S(2)}) collective-permute-start(f32[256,768]{1,0:T(8,128)S(1)} %collective-permute-done.8.refs_3_), channel_id=1, source_target_pairs={{0,32},{1,33},{2,34},{3,35},{4,36},{5,37},{6,38},{7,39},{8,40},{9,... | collective-permute-start | bytes 2359304 | tf_op jit(solution)/shard_map/ppermute | solution.py:54
  82.9 3.4 %collective-permute-start.17 = (f32[256,768]{1,0:T(8,128)S(1)}, f32[256,768]{1,0:T(8,128)S(1)}, u32[]{:S(2)}, u32[]{:S(2)}) collective-permute-start(f32[256,768]{1,0:T(8,128)S(1)} %get-tuple-element.57), channel_id=1, source_target_pairs={{0,32},{1,33},{2,34},{3,35},{4,36},{5,37},{6,38},{7,39},{8,40},{9,... | collective-permute-start | bytes 2359304 | tf_op jit(solution)/shard_map/ppermute | solution.py:54
  83.4 4.0 %collective-permute-start.18 = (f32[256,768]{1,0:T(8,128)S(1)}, f32[256,768]{1,0:T(8,128)S(1)}, u32[]{:S(2)}, u32[]{:S(2)}) collective-permute-start(f32[256,768]{1,0:T(8,128)S(1)} %get-tuple-element.59), channel_id=1, source_target_pairs={{0,32},{1,33},{2,34},{3,35},{4,36},{5,37},{6,38},{7,39},{8,40},{9,... | collective-permute-start | bytes 2359304 | tf_op jit(solution)/shard_map/ppermute | solution.py:54
  87.5 19.9 %collective-permute-start.19 = (f32[4,256,768]{2,1,0:T(8,128)S(1)}, f32[4,256,768]{2,1,0:T(8,128)S(1)}, u32[]{:S(2)}, u32[]{:S(2)}) collective-permute-start(f32[4,256,768]{2,1,0:T(8,128)S(1)} %get-tuple-element.60), channel_id=1, source_target_pairs={{0,32},{1,33},{2,34},{3,35},{4,36},{5,37},{6,38},{7,39},{8,40},{9,... | collective-permute-start | bytes 9437192 | tf_op jit(solution)/shard_map/ppermute | solution.py:54
  87.7 6.6 %collective-permute-start.23 = (f32[256,768]{1,0:T(8,128)S(1)}, f32[256,768]{1,0:T(8,128)S(1)}, u32[]{:S(2)}, u32[]{:S(2)}) collective-permute-start(f32[256,768]{1,0:T(8,128)S(1)} %get-tuple-element.65), channel_id=1, source_target_pairs={{0,32},{1,33},{2,34},{3,35},{4,36},{5,37},{6,38},{7,39},{8,40},{9,... | collective-permute-start | bytes 2359304 | tf_op jit(solution)/shard_map/ppermute | solution.py:54
  88.1 12.1 %collective-permute-start.20 = (f32[256,768]{1,0:T(8,128)S(1)}, f32[256,768]{1,0:T(8,128)S(1)}, u32[]{:S(2)}, u32[]{:S(2)}) collective-permute-start(f32[256,768]{1,0:T(8,128)S(1)} %add.45), channel_id=1, source_target_pairs={{0,8},{1,9},{2,10},{3,11},{4,12},{5,13},{6,14},{7,15},{8,0},{9,1},... | collective-permute-start | bytes 2359304 | tf_op jit(solution)/shard_map/ppermute | solution.py:58
  88.7 12.1 %collective-permute-start.21 = (f32[256,768]{1,0:T(8,128)S(1)}, f32[256,768]{1,0:T(8,128)S(1)}, u32[]{:S(2)}, u32[]{:S(2)}) collective-permute-start(f32[256,768]{1,0:T(8,128)S(1)} %add.46), channel_id=1, source_target_pairs={{0,1},{1,0},{2,3},{3,2},{4,5},{5,4},{6,7},{7,6},{8,9},{9,8},{10,11... | collective-permute-start | bytes 2359304 | tf_op jit(solution)/shard_map/ppermute | solution.py:58
  90.2 12.1 %collective-permute-start.22 = (f32[256,768]{1,0:T(8,128)S(1)}, f32[256,768]{1,0:T(8,128)S(1)}, u32[]{:S(2)}, u32[]{:S(2)}) collective-permute-start(f32[256,768]{1,0:T(8,128)S(1)} %add.47), channel_id=1, source_target_pairs={{0,2},{1,3},{2,0},{3,1},{4,6},{5,7},{6,4},{7,5},{8,10},{9,11},{10,... | collective-permute-start | bytes 2359304 | tf_op jit(solution)/shard_map/ppermute | solution.py:58
  102.3 27.3 %collective-permute-start.24 = (f32[256,768]{1,0:T(8,128)}, f32[256,768]{1,0:T(8,128)}, u32[]{:S(2)}, u32[]{:S(2)}) collective-permute-start(f32[256,768]{1,0:T(8,128)} %add.50), channel_id=1, source_target_pairs={{0,11},{1,10},{2,9},{3,8},{4,15},{5,14},{6,13},{7,12},{8,3},{9,2},... | collective-permute-start | bytes 2359304 | tf_op jit(solution)/shard_map/ppermute | solution.py:309
  109.8 19.8 %collective-permute-start.27 = (f32[256,768]{1,0:T(8,128)}, f32[256,768]{1,0:T(8,128)}, u32[]{:S(2)}, u32[]{:S(2)}) collective-permute-start(f32[256,768]{1,0:T(8,128)} %get-tuple-element.71), channel_id=1, source_target_pairs={{0,2},{1,3},{2,0},{3,1},{4,6},{5,7},{6,4},{7,5},{8,10},{9,11},{10,... | collective-permute-start | bytes 2359304 | tf_op jit(solution)/shard_map/ppermute | solution.py:58
  110.0 19.6 %collective-permute-start.26 = (f32[256,768]{1,0:T(8,128)}, f32[256,768]{1,0:T(8,128)}, u32[]{:S(2)}, u32[]{:S(2)}) collective-permute-start(f32[256,768]{1,0:T(8,128)} %get-tuple-element.72), channel_id=1, source_target_pairs={{0,8},{1,9},{2,10},{3,11},{4,12},{5,13},{6,14},{7,15},{8,0},{9,1},... | collective-permute-start | bytes 2359304 | tf_op jit(solution)/shard_map/ppermute | solution.py:58
  110.7 18.9 %collective-permute-start.25 = (f32[256,768]{1,0:T(8,128)}, f32[256,768]{1,0:T(8,128)}, u32[]{:S(2)}, u32[]{:S(2)}) collective-permute-start(f32[256,768]{1,0:T(8,128)} %get-tuple-element.73), channel_id=1, source_target_pairs={{0,1},{1,0},{2,3},{3,2},{4,5},{5,4},{6,7},{7,6},{8,9},{9,8},{10,11... | collective-permute-start | bytes 2359304 | tf_op jit(solution)/shard_map/ppermute | solution.py:58
  (8 other events, 25.6 us)

commit v3 on v2

--- a/solution.py
+++ b/solution.py
@@ -16,6 +16,7 @@
 E = 768
 CHUNKS = 8
 NEAR = 4
+CUTS = ((0, 88), (88, 176), (176, 256))
 HALF = NEAR * ROWS
 SUB = 256
 MIB = 1024 * 1024
@@ -79,11 +80,12 @@
     return jnp.sum(x.reshape(-1, 8, x.shape[-1]), axis=0)
 
 
-def prep_images(c, d_refs, e_refs, hi_ref, lo_ref):
-    for k in range(NEAR):
-        hi, lo = split(unit(jnp.where(c == 0, d_refs[k][:ROWS], e_refs[k][ROWS:])))
-        hi_ref[pl.ds(k * ROWS, ROWS)] = hi
-        lo_ref[pl.ds(k * ROWS, ROWS)] = lo
+def prep_images(c, d_refs, e_refs, hi_ref, lo_ref, first=0):
+    for k, (d_ref, e_ref) in enumerate(zip(d_refs, e_refs)):
+        hi, lo = split(unit(jnp.where(c == 0, d_ref[:ROWS], e_ref[ROWS:])))
+        rows = pl.ds((first + k) * ROWS, ROWS)
+        hi_ref[rows] = hi
+        lo_ref[rows] = lo
 
 
 def prep_text(c, d_ref, e_ref, hi_ref, lo_ref, k):
@@ -184,19 +186,31 @@
             p_txt[2 * i + h] = out[h]
 
 
+def prep_kernel(core, *refs):
+    n = NEAR - 1
+    d_refs, e_refs, (ih, il, th, tl) = refs[:n], refs[n : 2 * n], refs[2 * n :]
+    prep_images(core[0], d_refs, e_refs, ih, il)
+    for k in range(n):
+        prep_text(core[0], d_refs[k], e_refs[k], th, tl, k)
+
+
 def rest_kernel(par, core, *refs):
-    d_refs, e_refs = refs[:NEAR], refs[NEAR : 2 * NEAR]
-    p_txt, p_img, ihn, iln, thn, tln, i_sums = refs[2 * NEAR : 2 * NEAR + 7]
-    outs = refs[2 * NEAR + 7 :]
+    d_last, e_last, *mid = refs[:6]
+    p_txt, p_img, ihn, iln, thn, tln, i_sums = refs[6:13]
+    outs = refs[13:]
     keep_far, send_far = outs[:NEAR], outs[NEAR : 2 * NEAR]
-    keep_near, send_near, line, ihf, ilf, thf, tlf, pin, pif, sums = outs[2 * NEAR :]
+    keep_own, send_own, keep_three, send_three, line, ihf, ilf, thf, tlf, pin, pif, sums = outs[2 * NEAR :]
+    keep_near = [keep_own] + [keep_three.at[k] for k in range(NEAR - 1)]
+    send_near = [send_own] + [send_three.at[k] for k in range(NEAR - 1)]
     c = core[0]
+    last = NEAR - 1
     pin[...] = p_img[...]
     pif[...] = jnp.zeros_like(pif)
     sums[...] = i_sums[...]
-    prep_images(c, d_refs, e_refs, ihf, ilf)
-    for k in range(NEAR):
-        prep_text(c, d_refs[k], e_refs[k], thf, tlf, k)
+    for src, dest in zip(mid, (ihf, ilf, thf, tlf)):
+        dest[: src.shape[0]] = src[...]
+    prep_images(c, [d_last], [e_last], ihf, ilf, last)
+    prep_text(c, d_last, e_last, thf, tlf, last)
 
     def put(keep, send, total):
         @pl.when(c == 0)
@@ -212,8 +226,12 @@
         ts = [(thn[2 * i + h], tln[2 * i + h]) for h in range(2)]
         tasks = [(h, ihf, ilf, pif, m * SUB) for h in range(2) for m in range(HALF // SUB)]
         out = work(par, ts, tasks, None, sums, [p_txt[2 * i], p_txt[2 * i + 1]])
-        for h in range(2):
-            put(keep_near.at[2 * i + h], send_near.at[2 * i + h], out[h])
+        for v in range(NEAR // 2):
+
+            @pl.when(i == v)
+            def _():
+                for h in range(2):
+                    put(keep_near[2 * v + h], send_near[2 * v + h], out[h])
 
     @pl.loop(0, NEAR)
     def _(k):
@@ -236,14 +254,14 @@
     @pl.when(c == 0)
     def _():
         for k in range(NEAR):
-            for src, dest in ((pin, keep_near.at[k]), (pif, keep_far[k])):
+            for src, dest in ((pin, keep_near[k]), (pif, keep_far[k])):
                 dest[:ROWS] = src[pl.ds(k * ROWS, ROWS)]
                 dest[ROWS:] = blank
 
     @pl.when(c == 1)
     def _():
         for k in range(NEAR):
-            for src, dest in ((pin, send_near.at[k]), (pif, send_far[k])):
+            for src, dest in ((pin, send_near[k]), (pif, send_far[k])):
                 dest[:ROWS] = blank
                 dest[ROWS:] = src[pl.ds(k * ROWS, ROWS)]
 
@@ -252,6 +270,7 @@
 VMEM = pl.BlockSpec(memory_space=pltpu.VMEM)
 SUMS = jax.ShapeDtypeStruct((3, 8, UNIT), F32)
 CHUNK = jax.ShapeDtypeStruct((UNIT, E), F32)
+THREE = jax.ShapeDtypeStruct((NEAR - 1, UNIT, E), F32)
 FOUR = jax.ShapeDtypeStruct((NEAR, UNIT, E), F32)
 
 
@@ -273,28 +292,42 @@
     )(par, core, *ds, *es)
 
 
-def rest_block(par, core, ds, es, before):
+def prep_block(core, ds, es):
+    n = NEAR - 1
+    image = jax.ShapeDtypeStruct((n * ROWS, E), BF16)
+    text = jax.ShapeDtypeStruct((n, UNIT, E), BF16)
+    return pl.pallas_call(
+        prep_kernel,
+        out_shape=(image, image, text, text),
+        in_specs=[SMEM] + [VMEM] * (2 * n),
+        out_specs=(VMEM,) * 4,
+        compiler_params=pltpu.CompilerParams(vmem_limit_bytes=16 * MIB),
+        cost_estimate=cost(0),
+        name="prep_block",
+    )(core, *ds, *es)
+
+
+def rest_block(par, core, arrays):
     image = pltpu.VMEM((HALF, E), BF16)
     text = pltpu.VMEM((NEAR, UNIT, E), BF16)
     return pl.pallas_call(
         rest_kernel,
-        out_shape=(CHUNK,) * (2 * NEAR) + (FOUR, FOUR, jax.ShapeDtypeStruct((128, 128), F32)),
-        in_specs=[SMEM, SMEM] + [VMEM] * (2 * NEAR + 7),
-        out_specs=(VMEM,) * (2 * NEAR + 3),
+        out_shape=(CHUNK,) * (2 * NEAR + 2) + (THREE, THREE, jax.ShapeDtypeStruct((128, 128), F32)),
+        in_specs=[SMEM, SMEM] + [VMEM] * len(arrays),
+        out_specs=(VMEM,) * (2 * NEAR + 5),
         scratch_shapes=[image, image, text, text, pltpu.VMEM((HALF, E), F32), pltpu.VMEM((HALF, E), F32), pltpu.VMEM((3, 8, UNIT), F32)],
         compiler_params=pltpu.CompilerParams(vmem_limit_bytes=24 * MIB),
         cost_estimate=cost((CHUNKS * CHUNKS - NEAR * NEAR) * ROWS * UNIT),
         name="rest_block",
-    )(par, core, *ds, *es, *before)
-
-
-def small(kernel, scalars, arrays, rows, name):
-    shape = jax.ShapeDtypeStruct((rows, E), F32)
+    )(par, core, *arrays)
+
+
+def small(kernel, scalars, arrays, rows, name, outs=2):
     return pl.pallas_call(
         kernel,
-        out_shape=(shape, shape),
+        out_shape=(jax.ShapeDtypeStruct((rows, E), F32),) * outs,
         in_specs=[SMEM] * len(scalars) + [VMEM] * len(arrays),
-        out_specs=(VMEM, VMEM),
+        out_specs=(VMEM,) * outs,
         compiler_params=pltpu.CompilerParams(vmem_limit_bytes=8 * MIB),
         cost_estimate=cost(0),
         name=name,
@@ -313,8 +346,8 @@
     return lax.optimization_barrier((a, *others))[0]
 
 
-def all_sum(line):
-    return jnp.sum(lax.all_to_all(line, AXES, 0, 0, tiled=True), axis=0)
+def exchange(line, axes):
+    return jnp.sum(lax.all_to_all(line, axes, 0, 0, tiled=True), axis=0, keepdims=True)
 
 
 def body(image_embed, text_embed, log_temp, bias):
@@ -328,27 +361,31 @@
     own = jnp.concatenate([jnp.where(first, image_embed, txt_rec), jnp.where(first, img_rec, text_embed)])
     e_own = jnp.concatenate([jnp.where(first, text_embed, img_rec), jnp.where(first, txt_rec, image_embed)])
     one = [swap(d, own) for d in range(3)]
-    last = corner(after(own, *one))
     zx = swap(0, one[2])
     yz = swap(2, one[1])
     xy = swap(1, one[0])
     near, e_near = [own] + one, [e_own] + [other_core(after(a, *one)) for a in one]
     before = near_block(par, core, near, e_near)
-    rest = [xy, yz, zx, last]
-    e_rest = [other_core(after(a, before[-1], *rest)) for a in rest]
-    outs = rest_block(par, core, rest, e_rest, before)
-    keep, send, (keep_near, send_near, line) = outs[:NEAR], outs[NEAR : 2 * NEAR], outs[2 * NEAR :]
+    two = [after(a, before[-1]) for a in (xy, yz, zx)]
+    last = jnp.concatenate([swap(d, a[lo:hi]) for d, a, (lo, hi) in zip((2, 0, 1), two, CUTS)])
+    rest = [*two, last]
+    e_rest = [other_core(after(a, *two)) for a in two] + [other_core(last)]
+    mid = prep_block(core, rest[:3], e_rest[:3])
+    outs = rest_block(par, core, [rest[3], e_rest[3], *mid, *before])
+    keep, send, (keep_own, send_own, keep_near, send_near, line) = outs[:NEAR], outs[NEAR : 2 * NEAR], outs[2 * NEAR :]
+    q_own = keep_own + other_core(send_own)
     q = [k + other_core(s) for k, s in zip(keep, send)]
     got = other_core(after(send_near, *q[:3]))
-    q_near = [keep_near[k] + got[k] for k in range(NEAR)]
+    q_near = [keep_near[k] + got[k] for k in range(NEAR - 1)]
     two = [swap(d, a) for a, d in zip(q[:3], (1, 2, 0))]
     far = corner(after(q[3], *two))
-    line = all_sum(after(line, *two))
-    one = [swap(d, q_near[d + 1] + two[d]) for d in (2, 1, 0)]
-    mine, theirs = small(total_kernel, (core,), (after(q_near[0], line), far, *one), ROWS, "total")
+    line = exchange(after(line, *two), AXES)
+    core_b, line = lax.optimization_barrier((core, line))
+    one = [swap(d, q_near[d] + two[d]) for d in (2, 1, 0)]
+    mine, theirs = small(total_kernel, (core_b,), (q_own, far, *one), ROWS, "total")
     theirs = other_core(theirs)
     d_image, d_text = small(grad_kernel, (par, core), (image_embed, text_embed, mine, theirs), ROWS, "grad")
-    return d_image, d_text, line[:3] / total
+    return d_image, d_text, line[0, :3] / total
 
 
 def solution(mesh):

time: 136 us -> 133 us (0.978)
  blocking collectives: 16 us -> 0 us
  waiting for transfers between devices: 32.9 us -> 39.5 us
  starting transfers between devices: 33.7 us -> 40 us
    all_to_all x1 -> x0, blocking collectives: 16 us -> none  [all_sum(): return jnp.sum(lax.all_to_all(line, AXES, 0, 0, tiled=True), axis=0)]
    all_to_all x0 -> x1, waiting for transfers between devices: none -> 10.2 us  [exchange(): lax.all_to_all(line, axes, 0, 0, tiled=True)]
    ppermute x12 -> x15, starting transfers between devices: 20.1 us -> 25.9 us  [swap(): return lax.ppermute(a, AXES, across(dim))]
    all_to_all x0 -> x1, starting transfers between devices: none -> 5.43 us  [exchange(): lax.all_to_all(line, axes, 0, 0, tiled=True)]
    ppermute x15 -> x16, waiting for transfers between devices: 12.4 us -> 7.63 us  [other_core(): return lax.ppermute(a, AXES, pairs(lambda c, x, y, z: (1 - c, x, y, z)))]
    ppermute x2 -> x1, starting transfers between devices: 8.53 us -> 3.9 us  [corner(): return lax.ppermute(a, AXES, pairs(move))]
    ppermute x12 -> x15, waiting for transfers between devices: 20.5 us -> 21.8 us  [swap(): return lax.ppermute(a, AXES, across(dim))]
    pallas_call x3 -> x4, Pallas kernels: 31.7 us -> 32.6 us  [the longest x1 28.3 us: rest_block(): pl.pallas_call(rest_kernel, out_shape=(CHUNK,) * (2 * NEAR + 2) + (THREE,...]
  transfers between devices with their start and end apart: 29 -> 33, of which waited for: 18 -> 17; matrix products, arithmetic and copies ran while one was open for 5% -> 4% of each run, Pallas kernels for 8% -> 9%
where the time goes in v3:
time: 133 us
  Pallas kernels  43.9 us (33%)
  starting transfers between devices  40 us (30%)
  waiting for transfers between devices  39.5 us (30%)
  other arithmetic  7.03 us (5%)
  between operations  2.18 us (2%)
    pallas_call x1, Pallas kernels, rest_block(): pl.pallas_call(rest_kernel, out_shape=(CHUNK,) * (2 * NEAR + 2) + (THREE,...  28.3 us
    ppermute x15, starting transfers between devices, swap(): return lax.ppermute(a, AXES, across(dim))  25.9 us
    ppermute x15, waiting for transfers between devices, swap(): return lax.ppermute(a, AXES, across(dim))  21.8 us
    pallas_call x1, Pallas kernels, near_block(): pl.pallas_call(near_kernel, out_shape=(FOUR, jax.ShapeDtypeStruct((HALF,...  11.3 us
    all_to_all x1, waiting for transfers between devices, exchange(): lax.all_to_all(line, axes, 0, 0, tiled=True)  10.2 us
    ppermute x16, waiting for transfers between devices, other_core(): return lax.ppermute(a, AXES, pairs(lambda c, x, y, z: (1 - c, x, y, z)))  7.63 us
    all_to_all x1, starting transfers between devices, exchange(): lax.all_to_all(line, axes, 0, 0, tiled=True)  5.43 us
    ppermute x16, starting transfers between devices, other_core(): return lax.ppermute(a, AXES, pairs(lambda c, x, y, z: (1 - c, x, y, z)))  4.82 us
  transfers between devices with their start and end apart: 33, of which 17 were waited for; matrix products, arithmetic and copies ran while one was open for 4% of the time, Pallas kernels for 9%

profile of v3, /device:TPU:1, one launch (start us, length us, event | category | flops | bytes accessed | tf_op | source)
XLA Modules:
  0.0 132.8 jit_solution(12481648984746643067)
XLA Ops:
  0.6 1.5 %collective-permute-start.1 = (f32[128,768]{1,0:T(8,128)}, f32[128,768]{1,0:T(8,128)S(1)}, u32[]{:S(2)}, u32[]{:S(2)}) collective-permute-start(f32[128,768]{1,0:T(8,128)} %image.1), channel_id=1, source_target_pairs={{0,32},{1,33},{2,34},{3,35},{4,36},{5,37},{6,38},{7,39},{8,40},{9,... | collective-permute-start | bytes 1179656 | tf_op jit(solution)/shard_map/ppermute | solution.py:55
  5.9 3.9 %collective-permute-start.5 = (f32[256,768]{1,0:T(8,128)S(1)}, f32[256,768]{1,0:T(8,128)S(1)}, u32[]{:S(2)}, u32[]{:S(2)}) collective-permute-start(f32[256,768]{1,0:T(8,128)S(1)} %pad_maximum_fusion.refs_0_), channel_id=1, source_target_pairs={{0,1},{1,0},{2,3},{3,2},{4,5},{5,4},{6,7},{7,6},{8,9},{9,8},{10,11... | collective-permute-start | bytes 2359304 | tf_op jit(solution)/shard_map/ppermute | solution.py:59
  9.8 2.7 %collective-permute-start.4 = (f32[256,768]{1,0:T(8,128)S(1)}, f32[256,768]{1,0:T(8,128)S(1)}, u32[]{:S(2)}, u32[]{:S(2)}) collective-permute-start(f32[256,768]{1,0:T(8,128)S(1)} %pad_maximum_fusion.refs_0_), channel_id=1, source_target_pairs={{0,8},{1,9},{2,10},{3,11},{4,12},{5,13},{6,14},{7,15},{8,0},{9,1},... | collective-permute-start | bytes 2359304 | tf_op jit(solution)/shard_map/ppermute | solution.py:59
  12.5 2.5 %collective-permute-start.2 = (f32[256,768]{1,0:T(8,128)S(1)}, f32[256,768]{1,0:T(8,128)S(1)}, u32[]{:S(2)}, u32[]{:S(2)}) collective-permute-start(f32[256,768]{1,0:T(8,128)S(1)} %pad_maximum_fusion.refs_0_), channel_id=1, source_target_pairs={{0,2},{1,3},{2,0},{3,1},{4,6},{5,7},{6,4},{7,5},{8,10},{9,11},{10,... | collective-permute-start | bytes 2359304 | tf_op jit(solution)/shard_map/ppermute | solution.py:59
  15.0 4.2 %collective-permute-done.5.refs_3_ = f32[256,768]{1,0:T(8,128)S(1)} collective-permute-done((f32[256,768]{1,0:T(8,128)S(1)}, f32[256,768]{1,0:T(8,128)S(1)}, u32[]{:S(2)}, u32[]{:S(2)}) %collective-permute-start.5) | collective-permute-done | bytes 786464 | tf_op jit(solution)/shard_map/ppermute | solution.py:59
  19.2 2.7 %collective-permute-done.4.refs_2_ = f32[256,768]{1,0:T(8,128)S(1)} collective-permute-done((f32[256,768]{1,0:T(8,128)S(1)}, f32[256,768]{1,0:T(8,128)S(1)}, u32[]{:S(2)}, u32[]{:S(2)}) %collective-permute-start.4) | collective-permute-done | bytes 786464 | tf_op jit(solution)/shard_map/ppermute | solution.py:59
  21.9 2.7 %collective-permute-done.2.refs_1_ = f32[256,768]{1,0:T(8,128)S(1)} collective-permute-done((f32[256,768]{1,0:T(8,128)S(1)}, f32[256,768]{1,0:T(8,128)S(1)}, u32[]{:S(2)}, u32[]{:S(2)}) %collective-permute-start.2) | collective-permute-done | bytes 786464 | tf_op jit(solution)/shard_map/ppermute | solution.py:59
  26.9 2.5 %collective-permute-start.12 = (f32[256,768]{1,0:T(8,128)S(1)}, f32[256,768]{1,0:T(8,128)S(1)}, u32[]{:S(2)}, u32[]{:S(2)}) collective-permute-start(f32[256,768]{1,0:T(8,128)S(1)} %collective-permute-done.5.refs_3_), channel_id=1, source_target_pairs={{0,2},{1,3},{2,0},{3,1},{4,6},{5,7},{6,4},{7,5},{8,10},{9,11},{10,... | collective-permute-start | bytes 2359304 | tf_op jit(solution)/shard_map/ppermute | solution.py:59
  30.8 11.3 %near_block.1 = (f32[4,256,768]{2,1,0:T(8,128)S(1)}, f32[512,768]{1,0:T(8,128)S(1)}, bf16[512,768]{1,0:T(8,128)(2,1)S(1)}, bf16[512,768]{1,0:T(8,128)(2,1)S(1)},...) custom-call(f32[2]{0:T(128)S(1)} %pad_maximum_fusion.2.par, ...), custom_call_target="tpu_custom_call" | custom-call | bytes 786432 | tf_op jit(solution)/shard_map/near_block/pallas_call | solution.py:284
  43.5 2.8 %collective-permute-start.13 = (f32[80,768]{1,0:T(8,128)S(1)}, f32[80,768]{1,0:T(8,128)S(1)}, u32[]{:S(2)}, u32[]{:S(2)}) collective-permute-start(f32[80,768]{1,0:T(8,128)S(1)} %slice.32), channel_id=1, source_target_pairs={{0,8},{1,9},{2,10},{3,11},{4,12},{5,13},{6,14},{7,15},{8,0},{9,1},... | collective-permute-start | bytes 737288 | tf_op jit(solution)/shard_map/ppermute | solution.py:59
  46.7 2.0 %collective-permute-done.9 = f32[88,768]{1,0:T(8,128)S(1)} collective-permute-done((f32[88,768]{1,0:T(8,128)S(1)}, f32[88,768]{1,0:T(8,128)S(1)}, u32[]{:S(2)}, u32[]{:S(2)}) %collective-permute-start.9) | collective-permute-done | bytes 270368 | tf_op jit(solution)/shard_map/ppermute | solution.py:59
  52.4 28.3 %rest_block.1 = (f32[256,768]{1,0:T(8,128)S(1)}, f32[256,768]{1,0:T(8,128)S(1)}, f32[256,768]{1,0:T(8,128)S(1)}, f32[256,768]{1,0:T(8,128)S(1)}, f32[256,768]{1,...) custom-call(f32[2]{0:T(128)S(1)} %pad_maximum_fusion.2.par, ...), custom_call_target="tpu_custom_call" | custom-call | bytes 786432 | tf_op jit(solution)/shard_map/rest_block/pallas_call | solution.py:313
  81.3 1.7 %collective-permute-done.18 = f32[256,768]{1,0:T(8,128)S(1)} collective-permute-done((f32[256,768]{1,0:T(8,128)S(1)}, f32[256,768]{1,0:T(8,128)S(1)}, u32[]{:S(2)}, u32[]{:S(2)}) %collective-permute-start.18) | collective-permute-done | bytes 786464 | tf_op jit(solution)/shard_map/ppermute | solution.py:55
  86.2 2.7 %collective-permute-start.19 = (f32[256,768]{1,0:T(8,128)S(1)}, f32[256,768]{1,0:T(8,128)S(1)}, u32[]{:S(2)}, u32[]{:S(2)}) collective-permute-start(f32[256,768]{1,0:T(8,128)S(1)} %add.42), channel_id=1, source_target_pairs={{0,8},{1,9},{2,10},{3,11},{4,12},{5,13},{6,14},{7,15},{8,0},{9,1},... | collective-permute-start | bytes 2359304 | tf_op jit(solution)/shard_map/ppermute | solution.py:59
  89.5 1.9 %collective-permute-start.23 = (f32[256,768]{1,0:T(8,128)S(1)}, f32[256,768]{1,0:T(8,128)S(1)}, u32[]{:S(2)}, u32[]{:S(2)}) collective-permute-start(f32[256,768]{1,0:T(8,128)S(1)} %add.44), channel_id=1, source_target_pairs={{0,2},{1,3},{2,0},{3,1},{4,6},{5,7},{6,4},{7,5},{8,10},{9,11},{10,... | collective-permute-start | bytes 2359304 | tf_op jit(solution)/shard_map/ppermute | solution.py:59
  92.4 5.8 %collective-permute-done.19 = f32[256,768]{1,0:T(8,128)S(1)} collective-permute-done((f32[256,768]{1,0:T(8,128)S(1)}, f32[256,768]{1,0:T(8,128)S(1)}, u32[]{:S(2)}, u32[]{:S(2)}) %collective-permute-start.19) | collective-permute-done | bytes 786464 | tf_op jit(solution)/shard_map/ppermute | solution.py:59
  98.2 2.7 %collective-permute-done.21 = f32[256,768]{1,0:T(8,128)S(1)} collective-permute-done((f32[256,768]{1,0:T(8,128)S(1)}, f32[256,768]{1,0:T(8,128)S(1)}, u32[]{:S(2)}, u32[]{:S(2)}) %collective-permute-start.21) | collective-permute-done | bytes 786464 | tf_op jit(solution)/shard_map/ppermute | solution.py:59
  101.6 3.9 %collective-permute-start.26 = (f32[256,768]{1,0:T(8,128)}, f32[256,768]{1,0:T(8,128)S(1)}, u32[]{:S(2)}, u32[]{:S(2)}) collective-permute-start(f32[256,768]{1,0:T(8,128)} %add.46), channel_id=1, source_target_pairs={{0,11},{1,10},{2,9},{3,8},{4,15},{5,14},{6,13},{7,12},{8,3},{9,2},... | collective-permute-start | bytes 2359304 | tf_op jit(solution)/shard_map/ppermute | solution.py:342
  105.5 1.6 %fusion.1 = (f32[256,768]{1,0:T(8,128)}, f32[256,768]{1,0:T(8,128)}, f32[256,768]{1,0:T(8,128)}) fusion(f32[256,768]{1,0:T(8,128)S(1)} %collective-permute-done.19, f32[3,256,768]{2,1,0:T(8,128)S(1)} %collective-permute-done.27, f32[3,256,768]{2,1,0:T(8,128)S(1)} %get-tuple-element.79, f32[256,768]{1,0:T(8,128)S(1)} %collective-permute-done.21, ...), kind=kLoop, calls=%fused_computation.2 | loop fusion | flops 1179648 | bytes 9437184 | tf_op jit(solution)/shard_map/add | solution.py:384
  107.2 2.7 %collective-permute-start.29 = (f32[256,768]{1,0:T(8,128)}, f32[256,768]{1,0:T(8,128)}, u32[]{:S(2)}, u32[]{:S(2)}) collective-permute-start(f32[256,768]{1,0:T(8,128)} %get-tuple-element.88), channel_id=1, source_target_pairs={{0,8},{1,9},{2,10},{3,11},{4,12},{5,13},{6,14},{7,15},{8,0},{9,1},... | collective-permute-start | bytes 2359304 | tf_op jit(solution)/shard_map/ppermute | solution.py:59
  110.6 5.4 %all-to-all-start = ((f32[128,1,128]{2,1,0:T(1,128)}), f32[128,1,128]{2,1,0:T(1,128)S(1)}, u32[]{:S(2)}, u32[]{:S(2)}) async-start(f32[128,1,128]{2,1,0:T(1,128)} %bitcast.2), calls=%async_computation | async-start | bytes 131072 | tf_op jit(solution)/shard_map/all_to_all | solution.py:350
  117.3 10.2 %all-to-all-done = f32[128,1,128]{2,1,0:T(1,128)S(1)} async-done(((f32[128,1,128]{2,1,0:T(1,128)}), f32[128,1,128]{2,1,0:T(1,128)S(1)}, u32[]{:S(2)}, u32[]{:S(2)}) %all-to-all-start) | async-done | bytes 65568 | tf_op jit(solution)/shard_map/all_to_all | solution.py:350
  127.6 1.6 %total.1 = (f32[128,768]{1,0:T(8,128)S(1)}, f32[128,768]{1,0:T(8,128)S(1)}) custom-call(s32[1]{0:T(128)} %bitcast.core, f32[256,768]{1,0:T(8,128)S(1)} %add.45.refs_0_, f32[256,768]{1,0:T(8,128)S(1)} %collective-permute-done.26.refs_1_, f32[256,768]{1,0:T(8,128)} %collective-permute-done.28.refs_2_, f32[256,768]{1,0:T(8,128)} %collective-permute-done.29.refs_3_, ...), custom_call_target="tpu_custom_call" | custom-call | bytes 786432 | tf_op jit(solution)/shard_map/total/pallas_call | solution.py:326
  131.1 1.7 %grad.1 = (f32[128,768]{1,0:T(8,128)}, f32[128,768]{1,0:T(8,128)}) custom-call(f32[2]{0:T(128)S(1)} %pad_maximum_fusion.2.par, s32[1]{0:T(128)} %bitcast.core, f32[128,768]{1,0:T(8,128)S(1)} %copy-done, f32[128,768]{1,0:T(8,128)S(1)} %copy-done.1, f32[128,768]{1,0:T(8,128)S(1)} %get-tuple-element.82.mine, f32[128,768]{1,0:T(8,128)S(1)} %collective-permute-done.31.theirs), custom_call_target="tpu_custom_call" | custom-call | bytes 786432 | tf_op jit(solution)/shard_map/grad/pallas_call | solution.py:326
  (70 shorter events, 21.8 us)
Async XLA Ops:
  5.9 13.3 %collective-permute-start.5 = (f32[256,768]{1,0:T(8,128)S(1)}, f32[256,768]{1,0:T(8,128)S(1)}, u32[]{:S(2)}, u32[]{:S(2)}) collective-permute-start(f32[256,768]{1,0:T(8,128)S(1)} %pad_maximum_fusion.refs_0_), channel_id=1, source_target_pairs={{0,1},{1,0},{2,3},{3,2},{4,5},{5,4},{6,7},{7,6},{8,9},{9,8},{10,11... | collective-permute-start | bytes 2359304 | tf_op jit(solution)/shard_map/ppermute | solution.py:59
  9.8 12.1 %collective-permute-start.4 = (f32[256,768]{1,0:T(8,128)S(1)}, f32[256,768]{1,0:T(8,128)S(1)}, u32[]{:S(2)}, u32[]{:S(2)}) collective-permute-start(f32[256,768]{1,0:T(8,128)S(1)} %pad_maximum_fusion.refs_0_), channel_id=1, source_target_pairs={{0,8},{1,9},{2,10},{3,11},{4,12},{5,13},{6,14},{7,15},{8,0},{9,1},... | collective-permute-start | bytes 2359304 | tf_op jit(solution)/shard_map/ppermute | solution.py:59
  12.5 12.1 %collective-permute-start.2 = (f32[256,768]{1,0:T(8,128)S(1)}, f32[256,768]{1,0:T(8,128)S(1)}, u32[]{:S(2)}, u32[]{:S(2)}) collective-permute-start(f32[256,768]{1,0:T(8,128)S(1)} %pad_maximum_fusion.refs_0_), channel_id=1, source_target_pairs={{0,2},{1,3},{2,0},{3,1},{4,6},{5,7},{6,4},{7,5},{8,10},{9,11},{10,... | collective-permute-start | bytes 2359304 | tf_op jit(solution)/shard_map/ppermute | solution.py:59
  24.6 6.2 %collective-permute-start.7 = (f32[256,768]{1,0:T(8,128)S(1)}, f32[256,768]{1,0:T(8,128)S(1)}, u32[]{:S(2)}, u32[]{:S(2)}) collective-permute-start(f32[256,768]{1,0:T(8,128)S(1)} %collective-permute-done.4.refs_2_), channel_id=1, source_target_pairs={{0,32},{1,33},{2,34},{3,35},{4,36},{5,37},{6,38},{7,39},{8,40},{9,... | collective-permute-start | bytes 2359304 | tf_op jit(solution)/shard_map/ppermute | solution.py:55
  25.1 5.7 %collective-permute-start.8 = (f32[256,768]{1,0:T(8,128)S(1)}, f32[256,768]{1,0:T(8,128)S(1)}, u32[]{:S(2)}, u32[]{:S(2)}) collective-permute-start(f32[256,768]{1,0:T(8,128)S(1)} %collective-permute-done.5.refs_3_), channel_id=1, source_target_pairs={{0,32},{1,33},{2,34},{3,35},{4,36},{5,37},{6,38},{7,39},{8,40},{9,... | collective-permute-start | bytes 2359304 | tf_op jit(solution)/shard_map/ppermute | solution.py:55
  25.1 17.0 %collective-permute-start.3 = (f32[256,768]{1,0:T(8,128)S(1)}, f32[256,768]{1,0:T(8,128)S(1)}, u32[]{:S(2)}, u32[]{:S(2)}) collective-permute-start(f32[256,768]{1,0:T(8,128)S(1)} %collective-permute-done.2.refs_1_), channel_id=1, source_target_pairs={{0,8},{1,9},{2,10},{3,11},{4,12},{5,13},{6,14},{7,15},{8,0},{9,1},... | collective-permute-start | bytes 2359304 | tf_op jit(solution)/shard_map/ppermute | solution.py:59
  25.1 18.1 %collective-permute-start.10 = (f32[256,768]{1,0:T(8,128)S(1)}, f32[256,768]{1,0:T(8,128)S(1)}, u32[]{:S(2)}, u32[]{:S(2)}) collective-permute-start(f32[256,768]{1,0:T(8,128)S(1)} %collective-permute-done.4.refs_2_), channel_id=1, source_target_pairs={{0,1},{1,0},{2,3},{3,2},{4,5},{5,4},{6,7},{7,6},{8,9},{9,8},{10,11... | collective-permute-start | bytes 2359304 | tf_op jit(solution)/shard_map/ppermute | solution.py:59
  26.9 16.6 %collective-permute-start.12 = (f32[256,768]{1,0:T(8,128)S(1)}, f32[256,768]{1,0:T(8,128)S(1)}, u32[]{:S(2)}, u32[]{:S(2)}) collective-permute-start(f32[256,768]{1,0:T(8,128)S(1)} %collective-permute-done.5.refs_3_), channel_id=1, source_target_pairs={{0,2},{1,3},{2,0},{3,1},{4,6},{5,7},{6,4},{7,5},{8,10},{9,11},{10,... | collective-permute-start | bytes 2359304 | tf_op jit(solution)/shard_map/ppermute | solution.py:59
  42.1 6.6 %collective-permute-start.9 = (f32[88,768]{1,0:T(8,128)S(1)}, f32[88,768]{1,0:T(8,128)S(1)}, u32[]{:S(2)}, u32[]{:S(2)}) collective-permute-start(f32[88,768]{1,0:T(8,128)S(1)} %slice.30), channel_id=1, source_target_pairs={{0,1},{1,0},{2,3},{3,2},{4,5},{5,4},{6,7},{7,6},{8,9},{9,8},{10,11... | collective-permute-start | bytes 811016 | tf_op jit(solution)/shard_map/ppermute | solution.py:59
  43.2 6.6 %collective-permute-start.11 = (f32[88,768]{1,0:T(8,128)S(1)}, f32[88,768]{1,0:T(8,128)S(1)}, u32[]{:S(2)}, u32[]{:S(2)}) collective-permute-start(f32[88,768]{1,0:T(8,128)S(1)} %slice.31), channel_id=1, source_target_pairs={{0,2},{1,3},{2,0},{3,1},{4,6},{5,7},{6,4},{7,5},{8,10},{9,11},{10,... | collective-permute-start | bytes 811016 | tf_op jit(solution)/shard_map/ppermute | solution.py:59
  43.5 6.3 %collective-permute-start.13 = (f32[80,768]{1,0:T(8,128)S(1)}, f32[80,768]{1,0:T(8,128)S(1)}, u32[]{:S(2)}, u32[]{:S(2)}) collective-permute-start(f32[80,768]{1,0:T(8,128)S(1)} %slice.32), channel_id=1, source_target_pairs={{0,8},{1,9},{2,10},{3,11},{4,12},{5,13},{6,14},{7,15},{8,0},{9,1},... | collective-permute-start | bytes 737288 | tf_op jit(solution)/shard_map/ppermute | solution.py:59
  46.2 3.9 %collective-permute-start.16 = (f32[256,768]{1,0:T(8,128)S(1)}, f32[256,768]{1,0:T(8,128)S(1)}, u32[]{:S(2)}, u32[]{:S(2)}) collective-permute-start(f32[256,768]{1,0:T(8,128)S(1)} %collective-permute-done.10.refs_1_), channel_id=1, source_target_pairs={{0,32},{1,33},{2,34},{3,35},{4,36},{5,37},{6,38},{7,39},{8,40},{9,... | collective-permute-start | bytes 2359304 | tf_op jit(solution)/shard_map/ppermute | solution.py:55
  81.2 4.0 %collective-permute-start.22 = (f32[256,768]{1,0:T(8,128)S(1)}, f32[256,768]{1,0:T(8,128)S(1)}, u32[]{:S(2)}, u32[]{:S(2)}) collective-permute-start(f32[256,768]{1,0:T(8,128)S(1)} %get-tuple-element.71), channel_id=1, source_target_pairs={{0,32},{1,33},{2,34},{3,35},{4,36},{5,37},{6,38},{7,39},{8,40},{9,... | collective-permute-start | bytes 2359304 | tf_op jit(solution)/shard_map/ppermute | solution.py:55
  85.3 20.1 %collective-permute-start.27 = (f32[3,256,768]{2,1,0:T(8,128)S(1)}, f32[3,256,768]{2,1,0:T(8,128)S(1)}, u32[]{:S(2)}, u32[]{:S(2)}) collective-permute-start(f32[3,256,768]{2,1,0:T(8,128)S(1)} %get-tuple-element.81), channel_id=1, source_target_pairs={{0,32},{1,33},{2,34},{3,35},{4,36},{5,37},{6,38},{7,39},{8,40},{9,... | collective-permute-start | bytes 7077896 | tf_op jit(solution)/shard_map/ppermute | solution.py:55
  85.8 5.6 %collective-permute-start.25 = (f32[256,768]{1,0:T(8,128)S(1)}, f32[256,768]{1,0:T(8,128)S(1)}, u32[]{:S(2)}, u32[]{:S(2)}) collective-permute-start(f32[256,768]{1,0:T(8,128)S(1)} %get-tuple-element.77), channel_id=1, source_target_pairs={{0,32},{1,33},{2,34},{3,35},{4,36},{5,37},{6,38},{7,39},{8,40},{9,... | collective-permute-start | bytes 2359304 | tf_op jit(solution)/shard_map/ppermute | solution.py:55
  86.2 12.1 %collective-permute-start.19 = (f32[256,768]{1,0:T(8,128)S(1)}, f32[256,768]{1,0:T(8,128)S(1)}, u32[]{:S(2)}, u32[]{:S(2)}) collective-permute-start(f32[256,768]{1,0:T(8,128)S(1)} %add.42), channel_id=1, source_target_pairs={{0,8},{1,9},{2,10},{3,11},{4,12},{5,13},{6,14},{7,15},{8,0},{9,1},... | collective-permute-start | bytes 2359304 | tf_op jit(solution)/shard_map/ppermute | solution.py:59
  88.8 12.1 %collective-permute-start.21 = (f32[256,768]{1,0:T(8,128)S(1)}, f32[256,768]{1,0:T(8,128)S(1)}, u32[]{:S(2)}, u32[]{:S(2)}) collective-permute-start(f32[256,768]{1,0:T(8,128)S(1)} %add.43), channel_id=1, source_target_pairs={{0,1},{1,0},{2,3},{3,2},{4,5},{5,4},{6,7},{7,6},{8,9},{9,8},{10,11... | collective-permute-start | bytes 2359304 | tf_op jit(solution)/shard_map/ppermute | solution.py:59
  89.5 12.1 %collective-permute-start.23 = (f32[256,768]{1,0:T(8,128)S(1)}, f32[256,768]{1,0:T(8,128)S(1)}, u32[]{:S(2)}, u32[]{:S(2)}) collective-permute-start(f32[256,768]{1,0:T(8,128)S(1)} %add.44), channel_id=1, source_target_pairs={{0,2},{1,3},{2,0},{3,1},{4,6},{5,7},{6,4},{7,5},{8,10},{9,11},{10,... | collective-permute-start | bytes 2359304 | tf_op jit(solution)/shard_map/ppermute | solution.py:59
  91.4 24.6 %collective-permute-start.24 = (f32[256,768]{1,0:T(8,128)S(1)}, f32[256,768]{1,0:T(8,128)}, u32[]{:S(2)}, u32[]{:S(2)}) collective-permute-start(f32[256,768]{1,0:T(8,128)S(1)} %get-tuple-element.75), channel_id=1, source_target_pairs={{0,32},{1,33},{2,34},{3,35},{4,36},{5,37},{6,38},{7,39},{8,40},{9,... | collective-permute-start | bytes 2359304 | tf_op jit(solution)/shard_map/ppermute | solution.py:55
  101.6 26.0 %collective-permute-start.26 = (f32[256,768]{1,0:T(8,128)}, f32[256,768]{1,0:T(8,128)S(1)}, u32[]{:S(2)}, u32[]{:S(2)}) collective-permute-start(f32[256,768]{1,0:T(8,128)} %add.46), channel_id=1, source_target_pairs={{0,11},{1,10},{2,9},{3,8},{4,15},{5,14},{6,13},{7,12},{8,3},{9,2},... | collective-permute-start | bytes 2359304 | tf_op jit(solution)/shard_map/ppermute | solution.py:342
  107.0 20.6 %collective-permute-start.30 = (f32[256,768]{1,0:T(8,128)}, f32[256,768]{1,0:T(8,128)S(1)}, u32[]{:S(2)}, u32[]{:S(2)}) collective-permute-start(f32[256,768]{1,0:T(8,128)} %get-tuple-element.87), channel_id=1, source_target_pairs={{0,2},{1,3},{2,0},{3,1},{4,6},{5,7},{6,4},{7,5},{8,10},{9,11},{10,... | collective-permute-start | bytes 2359304 | tf_op jit(solution)/shard_map/ppermute | solution.py:59
  107.2 20.4 %collective-permute-start.29 = (f32[256,768]{1,0:T(8,128)}, f32[256,768]{1,0:T(8,128)}, u32[]{:S(2)}, u32[]{:S(2)}) collective-permute-start(f32[256,768]{1,0:T(8,128)} %get-tuple-element.88), channel_id=1, source_target_pairs={{0,8},{1,9},{2,10},{3,11},{4,12},{5,13},{6,14},{7,15},{8,0},{9,1},... | collective-permute-start | bytes 2359304 | tf_op jit(solution)/shard_map/ppermute | solution.py:59
  109.9 17.7 %collective-permute-start.28 = (f32[256,768]{1,0:T(8,128)}, f32[256,768]{1,0:T(8,128)}, u32[]{:S(2)}, u32[]{:S(2)}) collective-permute-start(f32[256,768]{1,0:T(8,128)} %get-tuple-element.89), channel_id=1, source_target_pairs={{0,1},{1,0},{2,3},{3,2},{4,5},{5,4},{6,7},{7,6},{8,9},{9,8},{10,11... | collective-permute-start | bytes 2359304 | tf_op jit(solution)/shard_map/ppermute | solution.py:59
  110.6 16.8 %all-to-all-start = ((f32[128,1,128]{2,1,0:T(1,128)}), f32[128,1,128]{2,1,0:T(1,128)S(1)}, u32[]{:S(2)}, u32[]{:S(2)}) async-start(f32[128,1,128]{2,1,0:T(1,128)} %bitcast.2), calls=%async_computation | async-start | bytes 131072 | tf_op jit(solution)/shard_map/all_to_all | solution.py:350
  (11 other events, 51.8 us)
